TPU v7x, 32 devices: a whole 2x2x4 slice. The times are simulated.
32 devices in a mesh: gx: 8 (over z, y), gz: 4 (over x, core).
Axes of the slice: x: 2, y: 2, z: 4, core: 2. Of those that a mesh axis runs over, the one named last changes fastest.
Arguments:
- density: float32 [1024, 64, 128], P('gx', 'gz'), may hold values from 1 to 2
- momentum: float32 [3, 1024, 64, 128], P(None, 'gx', 'gz'), may hold values from -1 to 1
- energy: float32 [1024, 64, 128], P('gx', 'gz'), may hold values from 4 to 6
- metric: float32 [1024, 64, 128], P('gx', 'gz'), may hold values from 0.5 to 1.5
- deriv_matrix: float32 [1024, 1024], replicated, may hold values from -0.1875 to 0.1875
- smooth_matrix: float32 [1024, 1024], replicated, may hold values from -0.046875 to 0.046875
- panel_of_cell: int32 [1024, 64], P('gx', 'gz'), may hold values from 0 to 63, as said below
- shape_index: int32 [1024, 64], P('gx', 'gz'), may hold values from 0 to 255
- mode_table: float32 [256, 128], replicated, may hold values from -0.375 to 0.375
Outputs:
- new_density: float32 [1024, 64, 128], P('gx', 'gz')
- new_momentum: float32 [3, 1024, 64, 128], P(None, 'gx', 'gz')
- new_energy: float32 [1024, 64, 128], P('gx', 'gz')
- panel_forces: float32 [64, 128], P('gx')
Inputs may be any that keep to these rules, and one draw needn't show every extreme that they name: `panel_of_cell`: each of the 64 panels is one of 8 contiguous uneven runs of streamwise cells times one of 8 contiguous uneven runs of spanwise cells, panel number = run across the span * 8 + run along the stream; every panel has cells.
All inputs are finite; a program needn't handle non-finite values.
Results may differ from a plain program's by a relative error of at most 0.0003.
Values sent between devices are 32-bit elements; how exact they have to be, the bound alone decides.
A program may use at most 128 MiB of HBM per device.

v0:
```python
import jax
import jax.numpy as jnp
from jax import lax
from jax.sharding import PartitionSpec as P

NP = 64


time_step = 0.05
gas_factor = 0.4
pressure_ref = 2.0


def with_halo(cells, sides, width):
    for axis, dim in sides:
        count = lax.axis_size(axis)
        head = lax.slice_in_dim(cells, 0, width, axis=dim)
        tail = lax.slice_in_dim(cells, cells.shape[dim] - width, cells.shape[dim], axis=dim)
        cells = jnp.concatenate(
            [
                lax.ppermute(tail, axis, [(i, (i + 1) % count) for i in range(count)]),
                cells,
                lax.ppermute(head, axis, [((i + 1) % count, i) for i in range(count)]),
            ],
            axis=dim,
        )
    return cells


def pressure_of(state):
    kinetic = 0.5 * (state[1] * state[1] + state[2] * state[2] + state[3] * state[3]) / state[0]
    return gas_factor * (state[4] - kinetic)


def fluxes(state, direction):
    pressure = pressure_of(state)
    speed = state[1 + direction] / state[0]
    parts = [state[1 + direction]]
    for component in range(3):
        term = state[1 + component] * speed
        if component == direction:
            term = term + pressure
        parts.append(term)
    parts.append((state[4] + pressure) * speed)
    return jnp.stack(parts)


def slope_y(padded):
    return (
        8.0 * (padded[..., 3:-1] - padded[..., 1:-3]) - (padded[..., 4:] - padded[..., :-4])
    ) / 12.0


def along_y(field):
    return slope_y(jnp.pad(field, ((0, 0), (0, 0), (0, 0), (2, 2))))


def along_z(padded):
    return (
        8.0 * (padded[:, :, 3:-1] - padded[:, :, 1:-3]) - (padded[:, :, 4:] - padded[:, :, :-4])
    ) / 12.0


def span_slope(state):
    padded = with_halo(fluxes(state, 2), (("gz", 2),), 2)
    return along_z(padded)


def x_terms(state, deriv_matrix, smooth_matrix):
    flux = fluxes(state, 0)
    smooth = jnp.einsum("ij,kjzy->kizy", smooth_matrix, state, precision=lax.Precision.HIGHEST)
    slope = jnp.einsum("ij,kjzy->kizy", deriv_matrix, flux, precision=lax.Precision.HIGHEST)
    return smooth - slope


def rate(state, metric, deriv_matrix, smooth_matrix):
    pencil = lax.all_to_all(state, "gx", split_axis=2, concat_axis=1, tiled=True)
    across = lax.all_to_all(
        x_terms(pencil, deriv_matrix, smooth_matrix), "gx", split_axis=1, concat_axis=2, tiled=True
    )
    total = across - along_y(fluxes(state, 1)) - span_slope(state)
    return metric * total


def body(
    density,
    momentum,
    energy,
    metric,
    deriv_matrix,
    smooth_matrix,
    panel_of_cell,
    shape_index,
    mode_table,
):
    state = jnp.concatenate([density[None], momentum, energy[None]], axis=0)
    first = state + time_step * rate(state, metric, deriv_matrix, smooth_matrix)
    final = 0.5 * state + 0.5 * (
        first + time_step * rate(first, metric, deriv_matrix, smooth_matrix)
    )
    load = ((pressure_of(final[:, :, :, 0]) - pressure_ref) * metric[:, :, 0]).reshape(-1)
    panels = panel_of_cell.reshape(-1)
    shapes = shape_index.reshape(-1)
    shape_hits = (
        shapes[:, None] == jnp.arange(mode_table.shape[0], dtype=jnp.int32)[None, :]
    ).astype(jnp.float32)
    panel_hits = (panels[:, None] == jnp.arange(NP, dtype=jnp.int32)[None, :]).astype(jnp.float32)
    summed = jnp.dot(panel_hits.T, shape_hits * load[:, None], precision=lax.Precision.HIGHEST)
    partial_forces = jnp.dot(summed, mode_table, precision=lax.Precision.HIGHEST)
    owned = NP // lax.axis_size("gx")
    everything = lax.psum(partial_forces, ("gx", "gz"))
    forces = lax.dynamic_slice_in_dim(everything, lax.axis_index("gx") * owned, owned, 0)
    return (final[0], final[1:4], final[4], forces)


def solution(mesh):
    in_specs = (
        P("gx", "gz", None),
        P(None, "gx", "gz", None),
        P("gx", "gz", None),
        P("gx", "gz", None),
        P(),
        P(),
        P("gx", "gz"),
        P("gx", "gz"),
        P(),
    )
    out_specs = (P("gx", "gz", None), P(None, "gx", "gz", None), P("gx", "gz", None), P("gx", None))
    return jax.shard_map(body, mesh=mesh, in_specs=in_specs, out_specs=out_specs, check_vma=False)
```

profile of v0, /device:TPU:1, one launch (start us, length us, event | category | flops | bytes accessed | tf_op | source)
XLA Modules:
  0.0 797.4 jit_solution(16572814634397429909)
XLA Ops:
  3.3 2.8 copy.54
  8.8 4.5 pad_maximum_fusion.4
  13.3 6.3 copy.58
  19.5 121.3 %all_to_all.72 = f32[5,128,16,128]{3,1,0,2:T(8,128)} all-to-all(f32[5,128,16,128]{3,1,0,2:T(8,128)} %copy.58), channel_id=1, replica_groups=mesh['gx'=8,'gz'=4] {'gx'}, dimensions={2} | all-to-all | bytes 10485760 | tf_op jit(solution)/shard_map/all_to_all | solution.py:77
  140.8 6.1 copy.59
  146.9 4.9 fusion.60
  151.8 6.8 all_to_all.55
  172.8 4.3 add_dynamic-update-slice_fusion.3
  181.3 19.8 %fusion.26 = f32[5,2,128,1024]{3,2,1,0:T(8,128)S(1)} fusion(f32[5,1024,2,128]{1,3,2,0:T(8,128)} %multiply_dynamic-update-slice_fusion.9, f32[1024,1024]{1,0:T(8,128)S(1)} %copy-done.22), kind=kOutput, calls=%fused_computation.41 | convolution fusion | flops 16106127360 | bytes 14680064 | tf_op jit(solution)/shard_map/ij,kjzy->kizy/dot_general | solution.py:72
  201.1 19.6 %subtract_bitcast_fusion.1 = f32[5,1024,2,128]{1,3,2,0:T(8,128)} fusion(f32[5,2,128,1024]{3,2,1,0:T(8,128)S(1)} %fusion.26, f32[5,1024,2,128]{1,3,2,0:T(8,128)S(1)} %bitcast.179, f32[1024,1024]{1,0:T(8,128)S(1)} %copy-done.7), kind=kOutput, calls=%fused_computation.38 | convolution fusion | flops 16107438080 | bytes 19922944 | tf_op jit(solution)/shard_map/ij,kjzy->kizy/dot_general | solution.py:71
  220.6 8.8 %copy.60 = f32[5,1024,2,128]{3,2,0,1:T(2,128)} copy(f32[5,1024,2,128]{1,3,2,0:T(8,128)} %subtract_bitcast_fusion.1) | data formatting | bytes 10485760 | tf_op jit(solution)/shard_map/sub | solution.py:73
  229.4 4.7 all-to-all-start.1
  244.8 2.8 copy.57
  247.6 100.5 %all-to-all-done.1 = f32[5,1024,2,128]{3,2,0,1:T(2,128)} async-done(((f32[5,1024,2,128]{3,2,0,1:T(2,128)}), f32[5,1024,2,128]{3,2,0,1:T(2,128)}, u32[]{:S(2)}, u32[]{:S(2)}) %all-to-all-start.1) | async-done | bytes 5242912 | tf_op jit(solution)/shard_map/all_to_all | solution.py:78
  348.0 11.1 %copy.61 = f32[5,8,128,2,128]{2,3,1,4,0:T(2,128)} copy(f32[5,8,128,2,128]{4,3,0,2,1:T(2,128)} %bitcast.9) | data formatting | bytes 10485760 | tf_op jit(solution)/shard_map/all_to_all | solution.py:78
  359.1 20.2 %fusion.20 = f32[5,128,16,128]{1,2,3,0:T(8,128)} fusion(f32[5,128,2,128]{1,2,3,0:T(2,128)} %collective-permute-done.1, f32[5,128,16,128]{1,2,3,0:T(8,128)} %copy-done.13, f32[5,128,2,128]{1,2,3,0:T(2,128)} %collective-permute-done, f32[5,128,16,128]{1,2,3,0:T(8,128)} %bitcast.175, f32[5,128,16,128]{1,2,3,0:T(8,128)} %copy-done.17, f32[128,16,128]{0,1,2:T(8,128)} %copy.57, ...), kind=kLoop, calls=%fused_computation.28 | loop fusion | flops 27525120 | bytes 28573696 | tf_op jit(solution)/shard_map/add | solution.py:97
  379.4 6.3 copy.70
  385.6 120.5 %all_to_all.73 = f32[5,128,16,128]{3,1,0,2:T(8,128)} all-to-all(f32[5,128,16,128]{3,1,0,2:T(8,128)} %copy.70), channel_id=1, replica_groups=mesh['gx'=8,'gz'=4] {'gx'}, dimensions={2} | all-to-all | bytes 10485760 | tf_op jit(solution)/shard_map/all_to_all | solution.py:77
  506.1 6.1 copy.71
  512.2 4.9 fusion.58
  517.1 6.7 all_to_all.63
  537.9 4.4 add_dynamic-update-slice_fusion.2
  546.5 19.8 %fusion.24 = f32[5,2,128,1024]{3,2,1,0:T(8,128)S(1)} fusion(f32[5,1024,2,128]{1,3,2,0:T(8,128)} %multiply_dynamic-update-slice_fusion.6, f32[1024,1024]{1,0:T(8,128)S(1)} %copy-done.23), kind=kOutput, calls=%fused_computation.39 | convolution fusion | flops 16106127360 | bytes 14680064 | tf_op jit(solution)/shard_map/ij,kjzy->kizy/dot_general | solution.py:72
  566.3 19.7 %subtract_bitcast_fusion = f32[5,1024,2,128]{1,3,2,0:T(8,128)} fusion(f32[5,2,128,1024]{3,2,1,0:T(8,128)S(1)} %fusion.24, f32[5,1024,2,128]{1,3,2,0:T(8,128)S(1)} %bitcast.181, f32[1024,1024]{1,0:T(8,128)S(1)} %copy-done.8), kind=kOutput, calls=%fused_computation.37 | convolution fusion | flops 16107438080 | bytes 19922944 | tf_op jit(solution)/shard_map/ij,kjzy->kizy/dot_general | solution.py:71
  586.0 8.8 %copy.72 = f32[5,1024,2,128]{3,2,0,1:T(2,128)} copy(f32[5,1024,2,128]{1,3,2,0:T(8,128)} %subtract_bitcast_fusion) | data formatting | bytes 10485760 | tf_op jit(solution)/shard_map/sub | solution.py:73
  594.8 4.7 all-to-all-start.3
  603.0 3.0 add_dynamic-update-slice_fusion.1
  615.4 97.8 %all-to-all-done.3 = f32[5,1024,2,128]{3,2,0,1:T(2,128)} async-done(((f32[5,1024,2,128]{3,2,0,1:T(2,128)}), f32[5,1024,2,128]{3,2,0,1:T(2,128)}, u32[]{:S(2)}, u32[]{:S(2)}) %all-to-all-start.3) | async-done | bytes 5242912 | tf_op jit(solution)/shard_map/all_to_all | solution.py:78
  713.2 11.1 %copy.73 = f32[5,8,128,2,128]{2,3,1,4,0:T(2,128)} copy(f32[5,8,128,2,128]{4,3,0,2,1:T(2,128)} %bitcast.28) | data formatting | bytes 10485760 | tf_op jit(solution)/shard_map/all_to_all | solution.py:78
  724.3 20.8 %fusion.10 = f32[5,128,16,128]{1,2,3,0:T(8,128)S(1)} fusion(f32[5,128,16,128]{1,2,3,0:T(8,128)} %fusion.20, f32[5,128,2,128]{1,2,3,0:T(2,128)} %collective-permute-done.3, f32[5,128,16,128]{1,2,3,0:T(8,128)} %copy-done.14, f32[5,128,2,128]{1,2,3,0:T(2,128)} %collective-permute-done.2, f32[5,128,16,128]{1,2,3,0:T(8,128)} %bitcast.182, ...), kind=kLoop, calls=%fused_computation.18 | loop fusion | flops 30146560 | bytes 33816576 | tf_op jit(solution)/shard_map/add | solution.py:98
  749.2 2.8 copy.77
  757.0 39.4 %psum.7 = f32[64,128]{1,0:T(8,128)S(1)} all-reduce(f32[64,128]{1,0:T(8,128)S(1)} %fusion.62), channel_id=1, replica_groups=mesh['gx'=8,'gz'=4] {'gx','gz'}, use_global_device_ids=true, to_apply=%region_0.1 | all-reduce | flops 8192 | bytes 65536 | tf_op jit(solution)/shard_map/psum | solution.py:111
  (123 shorter events, 75.2 us)
Async XLA Ops:
  0.6 756.2 %copy-start = (f32[256,128]{1,0:T(8,128)S(1)}, f32[256,128]{1,0:T(8,128)}, u32[]{:S(2)}) copy-start(f32[256,128]{1,0:T(8,128)} %param.17) | copy-start | bytes 393220
  172.8 4.3 copy-start.3
  172.8 4.3 copy-start.5
  172.8 4.3 copy-start.9
  172.8 5.7 copy-start.10
  177.1 2.6 copy-start.16
  178.4 2.9 copy-start.22
  179.7 21.4 %slice-start.2 = ((s8[5242880]{0:T(1024)(128)(4,1)}), s8[4194304]{0:T(1024)(128)(4,1)S(1)}, s32[]{:S(2)}) async-start(s8[5242880]{0:T(1024)(128)(4,1)} %bitcast.178), calls=%async_computation.6 | async-start | bytes 8388608
  181.3 19.8 %slice-start.3 = ((s8[5242880]{0:T(1024)(128)(4,1)}), s8[1048576]{0:T(1024)(128)(4,1)S(1)}, s32[]{:S(2)}) async-start(s8[5242880]{0:T(1024)(128)(4,1)} %bitcast.178), calls=%async_computation.7 | async-start | bytes 2097152
  181.3 19.8 %copy-start.7 = (f32[1024,1024]{1,0:T(8,128)S(1)}, f32[1024,1024]{1,0:T(8,128)}, u32[]{:S(2)}) copy-start(f32[1024,1024]{1,0:T(8,128)} %param.14) | copy-start | bytes 12582916
  229.4 118.6 %all-to-all-start.1 = ((f32[5,1024,2,128]{3,2,0,1:T(2,128)}), f32[5,1024,2,128]{3,2,0,1:T(2,128)}, u32[]{:S(2)}, u32[]{:S(2)}) async-start(f32[5,1024,2,128]{3,2,0,1:T(2,128)} %copy.60), calls=%async_computation.1 | async-start | bytes 10485760 | tf_op jit(solution)/shard_map/all_to_all | solution.py:78
  237.2 4.3 copy-start.17
  241.5 117.6 %collective-permute-start = (f32[5,128,2,128]{1,2,3,0:T(2,128)}, f32[5,128,2,128]{1,2,3,0:T(2,128)}, u32[]{:S(2)}, u32[]{:S(2)}) collective-permute-start(f32[5,128,2,128]{1,2,3,0:T(2,128)} %get-tuple-element.42), channel_id=1, source_target_pairs={{1,0},{2,1},{3,2},{0,3},{5,4},{6,5},{7,6},{4,7},{9,8},{10,9},{11,1... | collective-permute-start | bytes 1966088 | tf_op jit(solution)/shard_map/ppermute | solution.py:23
  243.3 115.8 %collective-permute-start.1 = (f32[5,128,2,128]{1,2,3,0:T(2,128)}, f32[5,128,2,128]{1,2,3,0:T(2,128)}, u32[]{:S(2)}, u32[]{:S(2)}) collective-permute-start(f32[5,128,2,128]{1,2,3,0:T(2,128)} %get-tuple-element.43), channel_id=1, source_target_pairs={{0,1},{1,2},{2,3},{3,0},{4,5},{5,6},{6,7},{7,4},{8,9},{9,10},{10,1... | collective-permute-start | bytes 1966088 | tf_op jit(solution)/shard_map/ppermute | solution.py:21
  537.9 4.4 copy-start.4
  537.9 4.4 copy-start.6
  537.9 4.4 copy-start.11
  537.9 5.7 copy-start.12
  542.3 2.5 copy-start.15
  543.6 2.9 copy-start.23
  544.9 21.4 %slice-start.4 = ((s8[5242880]{0:T(1024)(128)(4,1)}), s8[4194304]{0:T(1024)(128)(4,1)S(1)}, s32[]{:S(2)}) async-start(s8[5242880]{0:T(1024)(128)(4,1)} %bitcast.180), calls=%async_computation.8 | async-start | bytes 8388608
  546.5 19.8 %slice-start.5 = ((s8[5242880]{0:T(1024)(128)(4,1)}), s8[1048576]{0:T(1024)(128)(4,1)S(1)}, s32[]{:S(2)}) async-start(s8[5242880]{0:T(1024)(128)(4,1)} %bitcast.180), calls=%async_computation.9 | async-start | bytes 2097152
  546.5 19.8 %copy-start.8 = (f32[1024,1024]{1,0:T(8,128)S(1)}, f32[1024,1024]{1,0:T(8,128)}, u32[]{:S(2)}) copy-start(f32[1024,1024]{1,0:T(8,128)} %param.14) | copy-start | bytes 12582916
  594.8 118.4 %all-to-all-start.3 = ((f32[5,1024,2,128]{3,2,0,1:T(2,128)}), f32[5,1024,2,128]{3,2,0,1:T(2,128)}, u32[]{:S(2)}, u32[]{:S(2)}) async-start(f32[5,1024,2,128]{3,2,0,1:T(2,128)} %copy.72), calls=%async_computation.3 | async-start | bytes 10485760 | tf_op jit(solution)/shard_map/all_to_all | solution.py:78
  600.8 5.2 slice-start
  603.0 3.0 slice-start.1
  606.9 4.4 copy-start.18
  606.9 7.7 copy-start.19
  606.9 8.1 %copy-start.20 = (s32[128,16]{0,1:T(8,128)S(1)}, s32[128,16]{0,1:T(8,128)}, u32[]{:S(2)}) copy-start(s32[128,16]{0,1:T(8,128)} %param.15) | copy-start | bytes 24580
  606.9 8.3 %copy-start.21 = (s32[128,16]{0,1:T(8,128)S(1)}, s32[128,16]{0,1:T(8,128)}, u32[]{:S(2)}) copy-start(s32[128,16]{0,1:T(8,128)} %param.16) | copy-start | bytes 24580
  611.3 113.0 %collective-permute-start.2 = (f32[5,128,2,128]{1,2,3,0:T(2,128)}, f32[5,128,2,128]{1,2,3,0:T(2,128)}, u32[]{:S(2)}, u32[]{:S(2)}) collective-permute-start(f32[5,128,2,128]{1,2,3,0:T(2,128)} %get-tuple-element.35), channel_id=1, source_target_pairs={{1,0},{2,1},{3,2},{0,3},{5,4},{6,5},{7,6},{4,7},{9,8},{10,9},{11,1... | collective-permute-start | bytes 1966088 | tf_op jit(solution)/shard_map/ppermute | solution.py:23
  613.3 111.0 %collective-permute-start.3 = (f32[5,128,2,128]{1,2,3,0:T(2,128)}, f32[5,128,2,128]{1,2,3,0:T(2,128)}, u32[]{:S(2)}, u32[]{:S(2)}) collective-permute-start(f32[5,128,2,128]{1,2,3,0:T(2,128)} %get-tuple-element.36), channel_id=1, source_target_pairs={{0,1},{1,2},{2,3},{3,0},{4,5},{5,6},{6,7},{7,4},{8,9},{9,10},{10,1... | collective-permute-start | bytes 1966088 | tf_op jit(solution)/shard_map/ppermute | solution.py:21
  (4 other events, 8.3 us)
where the time goes:
time: 807 us; the launch traced here: 797 us
  blocking collectives  281 us (35%)
  waiting for transfers between devices  198 us (25%)
  local copies, waits for them, and re-layouts  148 us (18%)
  matrix products  80.9 us (10%)
  other arithmetic  71.7 us (9%)
  starting transfers between devices  16 us (2%)
    all_to_all x2, blocking collectives, rate(): lax.all_to_all(state, 'gx', split_axis=2, concat_axis=1, tiled=True)  242 us
    all_to_all x2, waiting for transfers between devices, rate(): lax.all_to_all(x_terms(pencil, deriv_matrix, smooth_matrix), 'gx', split_...  198 us
    dot_general x2, matrix products, x_terms(): jnp.einsum('ij,kjzy->kizy', deriv_matrix, flux, precision=lax.Precision.H...  39.5 us
    psum x1, blocking collectives, body(): everything = lax.psum(partial_forces, ('gx', 'gz'))  39.4 us
    dot_general x2, matrix products, x_terms(): jnp.einsum('ij,kjzy->kizy', smooth_matrix, state, precision=lax.Precision...  39.2 us
    unnamed x73, local copies, waits for them, and re-layouts  29.9 us
    all_to_all x4, local copies, waits for them, and re-layouts, rate(): lax.all_to_all(state, 'gx', split_axis=2, concat_axis=1, tiled=True)  25.7 us
    all_to_all x2, local copies, waits for them, and re-layouts, rate(): lax.all_to_all(x_terms(pencil, deriv_matrix, smooth_matrix), 'gx', split_...  22.2 us
  transfers between devices with their start and end apart: 6, of which 2 were waited for; matrix products, arithmetic and copies ran while one was open for 5% of the time, Pallas kernels for 0%

commit v1 on v0

v1 whole, which is shorter than its diff:
```python
import functools

import jax
import jax.numpy as jnp
import numpy as np
from jax import lax
from jax.experimental import pallas as pl
from jax.experimental.pallas import tpu as pltpu
from jax.sharding import PartitionSpec as P

NP = 64

time_step = 0.05
gas_factor = 0.4
pressure_ref = 2.0

F32 = jnp.float32
BF16 = jnp.bfloat16
FIELDS = 5
LANES = 128
EDGE = 32
VMEM = 58 * 1024 * 1024


def params():
    return pltpu.CompilerParams(vmem_limit_bytes=VMEM)


def whole(count):
    return [pl.BlockSpec(memory_space=pltpu.VMEM)] * count


def ring_order(count):
    half = count // 2
    return [2 * p if p < half else 2 * (count - 1 - p) + 1 for p in range(count)]


def pressure_of(state):
    kinetic = 0.5 * (state[1] * state[1] + state[2] * state[2] + state[3] * state[3]) / state[0]
    return gas_factor * (state[4] - kinetic)


def flux_with(state, normal, hits):
    inverse = 1.0 / state[0]
    kinetic = 0.5 * (state[1] * state[1] + state[2] * state[2] + state[3] * state[3]) * inverse
    pressure = gas_factor * (state[4] - kinetic)
    speed = normal * inverse
    parts = [normal]
    for component in range(3):
        term = state[1 + component] * speed
        if hits[component] is True:
            term = term + pressure
        elif hits[component] is not False:
            term = term + jnp.where(hits[component], pressure, 0.0)
        parts.append(term)
    parts.append((state[4] + pressure) * speed)
    return parts


def flux(state, direction):
    return flux_with(state, state[1 + direction], [c == direction for c in range(3)])


def split2(value):
    high = value.astype(BF16)
    return high, (value - high.astype(F32)).astype(BF16)


def split3(value):
    high = value.astype(BF16)
    rest = value - high.astype(F32)
    middle = rest.astype(BF16)
    return high, middle, (rest - middle.astype(F32)).astype(BF16)


def swap_groups(rows, width):
    rows = list(rows)
    count = len(rows)
    shape = rows[0].shape
    axis = len(shape) - 1
    group = lax.broadcasted_iota(jnp.int32, shape, axis) // width
    bit = 1
    while bit < count:
        odd = (group // bit) % 2 == 1
        for k in range(count):
            if k & bit:
                continue
            a, b = rows[k], rows[k | bit]
            rows[k] = jnp.where(odd, pltpu.roll(b, bit * width, axis), a)
            rows[k | bit] = jnp.where(odd, b, pltpu.roll(a, LANES - bit * width, axis))
        bit *= 2
    return rows


def pack_kernel(count, z_cells, order, density, momentum, energy, metric, out):
    x_cells = out.shape[2]
    width = LANES // count
    sources = [density, momentum.at[0], momentum.at[1], momentum.at[2], energy, metric]

    @pl.loop(0, x_cells // 8)
    def _(chunk):
        row = pl.multiple_of(chunk * 8, 8)
        for field, source in enumerate(sources):
            for half in range(z_cells // count):
                planes = [
                    source[pl.ds(row * z_cells + half * count + k, 8, stride=z_cells), :] for k in range(count)
                ]
                tiles = swap_groups(planes, width)
                for t in range(count):
                    out[order[t], field, pl.ds(row, 8), half * LANES : (half + 1) * LANES] = tiles[t]


def unpack_kernel(count, z_cells, order, packed, density, momentum, energy):
    x_cells = packed.shape[2]
    width = LANES // count
    targets = [density, momentum.at[0], momentum.at[1], momentum.at[2], energy]

    @pl.loop(0, x_cells // 8)
    def _(chunk):
        row = pl.multiple_of(chunk * 8, 8)
        for field, target in enumerate(targets):
            for half in range(z_cells // count):
                tiles = [
                    packed[order[t], field, pl.ds(row, 8), half * LANES : (half + 1) * LANES] for t in range(count)
                ]
                planes = swap_groups(tiles, width)
                for k in range(count):
                    target[pl.ds(row * z_cells + half * count + k, 8, stride=z_cells), :] = planes[k]


def matmul_kernel(q, deriv, smooth, out, left_high, left_low, right_high, right_low):
    blocks, _, x_cells, lanes = q.shape
    length = blocks * x_cells

    @pl.loop(0, length // 32)
    def _(chunk):
        row = pl.multiple_of(chunk * 32, 32)
        for column, matrix, sign in ((0, smooth, 1.0), (1, deriv, -1.0)):
            high, low = split2(sign * matrix[pl.ds(row, 32), :])
            left_high[pl.ds(row, 32), column * length : (column + 1) * length] = high
            left_low[pl.ds(row, 32), column * length : (column + 1) * length] = low

    step = 16
    for block in range(blocks):

        @pl.loop(0, x_cells // step)
        def _(chunk):
            row = pl.multiple_of(chunk * step, step)
            state = [q[block, f, pl.ds(row, step), :] for f in range(FIELDS)]
            flow = flux(state, 0)
            for f in range(FIELDS):
                for base, value in ((0, state[f]), (length, flow[f])):
                    high, low = split2(value)
                    at = pl.ds(pl.multiple_of(base + block * x_cells + row, step), step)
                    right_high[f, at, :] = high
                    right_low[f, at, :] = low

    tall = min(512, length)

    @pl.loop(0, length // tall)
    def _(part):
        row = pl.multiple_of(part * tall, tall)

        @pl.loop(0, FIELDS)
        def _(f):
            a = left_high[pl.ds(row, tall), :]
            b = right_high[f]
            total = jnp.dot(a, b, preferred_element_type=F32)
            total += jnp.dot(a, right_low[f], preferred_element_type=F32)
            total += jnp.dot(left_low[pl.ds(row, tall), :], b, preferred_element_type=F32)
            out[f, pl.ds(row, tall), :] = total


def edges_of(values, select):
    return sum(jnp.dot(part, select, preferred_element_type=F32) for part in split3(values))


def rows_of(quarter, row, blocks, x_cells):
    return quarter * (blocks // 4) + row // x_cells, pl.multiple_of(row % x_cells, 16)


def edge_kernel(q, select, out):
    blocks, _, x_cells, lanes = q.shape
    step = 32

    @pl.loop(0, blocks * x_cells // 4 // step)
    def _(chunk):
        row = pl.multiple_of(chunk * step, step)
        for f in range(FIELDS):
            edges = []
            for quarter in range(4):
                block, at = rows_of(quarter, row, blocks, x_cells)
                edges.append(edges_of(q[block, f, pl.ds(at, step), :], select[...]))
            for d, value in enumerate(swap_groups(edges, EDGE)):
                out[d, f, pl.ds(row, step), :] = value


def finish_kernel(second, *refs):
    if second:
        start, q, x_part, h0, h1, h2, h3, mask, weights, out, high, low = refs
        edges_out = None
    else:
        q, x_part, h0, h1, h2, h3, mask, weights, select, out, edges_out, high, low, made = refs
        start = q
    blocks, _, x_cells, lanes = q.shape
    step = 32
    quarter_rows = blocks * x_cells // 4

    @pl.loop(0, quarter_rows // step)
    def _(chunk):
        row = pl.multiple_of(chunk * step, step)
        halo = []
        for f in range(FIELDS):
            halo.append(swap_groups([h[f, pl.ds(row, step), :] for h in (h0, h1, h2, h3)], EDGE))
        lane = lax.broadcasted_iota(jnp.int32, (step, LANES), 1)
        wall = lane < 2 * EDGE
        inside = jnp.broadcast_to(mask[0:1, :], (step, LANES)) > 0.0
        for quarter in range(4):
            block, at = rows_of(quarter, row, blocks, x_cells)
            edge = [halo[f][quarter] for f in range(FIELDS)]
            edge_flux = flux_with(
                edge, jnp.where(wall, edge[2], edge[3]), [False, wall, jnp.logical_not(wall)]
            )
            state = [q[block, f, pl.ds(at, step), :] for f in range(FIELDS)]
            across, along = flux(state, 1), flux(state, 2)
            for f in range(FIELDS):
                base = (quarter * FIELDS + f) * step
                for left, value in (
                    (0, across[f]),
                    (lanes, along[f]),
                    (2 * lanes, jnp.where(inside, edge_flux[f], 0.0)),
                ):
                    top, rest = split2(value)
                    high[base : base + step, left : left + value.shape[1]] = top
                    low[base : base + step, left : left + value.shape[1]] = rest
        slopes = jnp.dot(high[...], weights[...], preferred_element_type=F32)
        slopes += jnp.dot(low[...], weights[...], preferred_element_type=F32)
        for quarter in range(4):
            block, at = rows_of(quarter, row, blocks, x_cells)
            scale = time_step * start[block, FIELDS, pl.ds(at, step), :]
            whole_row = pl.ds(pl.multiple_of(quarter * quarter_rows + row, step), step)
            for f in range(FIELDS):
                base = (quarter * FIELDS + f) * step
                total = x_part[f, whole_row, :] - slopes[base : base + step, :] * (1.0 / 12.0)
                value = q[block, f, pl.ds(at, step), :] + scale * total
                if second:
                    value = 0.5 * start[block, f, pl.ds(at, step), :] + 0.5 * value
                else:
                    made[base : base + step, :] = value
                out[block, f, pl.ds(at, step), :] = value
        if not second:
            edges = edges_of(made[...], select[...])
            for f in range(FIELDS):
                parts = [
                    edges[(r * FIELDS + f) * step : (r * FIELDS + f + 1) * step, :] for r in range(4)
                ]
                for d, value in enumerate(swap_groups(parts, EDGE)):
                    edges_out[d, f, pl.ds(row, step), :] = value


def tables(z_cells, y_cells):
    lanes = z_cells * y_cells
    select = np.zeros((lanes, LANES), np.float32)
    weights = np.zeros((2 * lanes + LANES, lanes), np.float32)
    for c in range(EDGE):
        a, z = (c // z_cells) % 2, c % z_cells
        select[z * y_cells + a, c] = 1
        select[z * y_cells + y_cells - 2 + a, EDGE + c] = 1
        a, y = (c // y_cells) % 2, c % y_cells
        select[a * y_cells + y, 2 * EDGE + c] = 1
        select[(z_cells - 2 + a) * y_cells + y, 3 * EDGE + c] = 1
    halo = 2 * lanes
    for z in range(z_cells):
        for y in range(y_cells):
            to = z * y_cells + y
            for off, factor in ((1, 8.0), (-1, -8.0), (2, -1.0), (-2, 1.0)):
                at = y + off
                if at < 0:
                    source = halo + (at + 2) * z_cells + z
                elif at >= y_cells:
                    source = halo + EDGE + (at - y_cells) * z_cells + z
                else:
                    source = z * y_cells + at
                weights[source, to] += factor
                at = z + off
                if at < 0:
                    source = halo + 2 * EDGE + (at + 2) * y_cells + y
                elif at >= z_cells:
                    source = halo + 3 * EDGE + (at - z_cells) * y_cells + y
                else:
                    source = lanes + at * y_cells + y
                weights[source, to] += factor
    return jnp.asarray(select, BF16), jnp.asarray(weights, BF16)


def exchange(edges, order):
    count = len(order)
    spans = lax.axis_size("gz")
    down = [(order[p], order[(p - 1) % count]) for p in range(count)]
    up = [(order[p], order[(p + 1) % count]) for p in range(count)]
    left = [(i, (i - 1) % spans) for i in range(spans)]
    right = [(i, (i + 1) % spans) for i in range(spans)]
    return (
        lax.ppermute(edges[1], "gx", up),
        lax.ppermute(edges[0], "gx", down),
        lax.ppermute(edges[3], "gz", right),
        lax.ppermute(edges[2], "gz", left),
    )


def cost(flops, moved):
    return pl.CostEstimate(flops=flops, bytes_accessed=moved, transcendentals=0)


def body(
    density,
    momentum,
    energy,
    metric,
    deriv_matrix,
    smooth_matrix,
    panel_of_cell,
    shape_index,
    mode_table,
):
    count = lax.axis_size("gx")
    order = ring_order(count)
    x_cells, z_cells, y_cells = density.shape
    tile_y = y_cells // count
    lanes = z_cells * tile_y
    length = count * x_cells
    flat = (x_cells * z_cells, y_cells)
    select, weights = tables(z_cells, tile_y)

    packed = pl.pallas_call(
        functools.partial(pack_kernel, count, z_cells, order),
        out_shape=jax.ShapeDtypeStruct((count, FIELDS + 1, x_cells, lanes), F32),
        in_specs=whole(4),
        out_specs=whole(1)[0],
        compiler_params=params(),
    )(density.reshape(flat), momentum.reshape((3,) + flat), energy.reshape(flat), metric.reshape(flat))
    start = lax.all_to_all(packed, "gx", split_axis=0, concat_axis=0, tiled=True)

    def x_terms(state):
        return pl.pallas_call(
            matmul_kernel,
            out_shape=jax.ShapeDtypeStruct((FIELDS, length, lanes), F32),
            in_specs=whole(3),
            out_specs=whole(1)[0],
            scratch_shapes=[pltpu.VMEM((length, 2 * length), BF16)] * 2
            + [pltpu.VMEM((FIELDS, 2 * length, lanes), BF16)] * 2,
            compiler_params=params(),
            cost_estimate=cost(12 * FIELDS * length * length * lanes, 40 * FIELDS * length * lanes),
        )(state, deriv_matrix, smooth_matrix)

    edge_shape = jax.ShapeDtypeStruct((4, FIELDS, length // 4, LANES), F32)
    place = jnp.asarray(order, jnp.int32)
    tile = jnp.argmax(place == lax.axis_index("gx"))
    lane = lax.broadcasted_iota(jnp.int32, (8, LANES), 1)
    beyond = ((tile == 0) & (lane < EDGE)) | ((tile == count - 1) & (lane >= EDGE) & (lane < 2 * EDGE))
    mask = jnp.where(beyond, 0.0, 1.0).astype(F32)

    edges = pl.pallas_call(
        edge_kernel,
        out_shape=edge_shape,
        in_specs=whole(2),
        out_specs=whole(1)[0],
        compiler_params=params(),
    )(start, select)
    halo = exchange(edges, order)
    split_rows = [pltpu.VMEM((4 * FIELDS * 32, 2 * lanes + LANES), BF16)] * 2
    first, edges = pl.pallas_call(
        functools.partial(finish_kernel, False),
        out_shape=(jax.ShapeDtypeStruct((count, FIELDS, x_cells, lanes), F32), edge_shape),
        in_specs=whole(9),
        out_specs=tuple(whole(2)),
        scratch_shapes=split_rows + [pltpu.VMEM((4 * FIELDS * 32, lanes), F32)],
        compiler_params=params(),
    )(start, x_terms(start), *halo, mask, weights, select)
    halo = exchange(edges, order)
    final = pl.pallas_call(
        functools.partial(finish_kernel, True),
        out_shape=jax.ShapeDtypeStruct((count, FIELDS, x_cells, lanes), F32),
        in_specs=whole(9),
        out_specs=whole(1)[0],
        scratch_shapes=split_rows,
        compiler_params=params(),
    )(start, first, x_terms(first), *halo, mask, weights)
    back = lax.all_to_all(final, "gx", split_axis=0, concat_axis=0, tiled=True)
    new_density, new_momentum, new_energy = pl.pallas_call(
        functools.partial(unpack_kernel, count, z_cells, order),
        out_shape=(
            jax.ShapeDtypeStruct(flat, F32),
            jax.ShapeDtypeStruct((3,) + flat, F32),
            jax.ShapeDtypeStruct(flat, F32),
        ),
        in_specs=whole(1),
        out_specs=tuple(whole(3)),
        compiler_params=params(),
    )(back)

    floor = back[order[0]].reshape(FIELDS, x_cells, z_cells, tile_y)[..., 0]
    load = ((pressure_of(floor) - pressure_ref) * metric[:, :, 0]).reshape(-1)
    panels = panel_of_cell.reshape(-1)
    shapes = shape_index.reshape(-1)
    shape_hits = (
        shapes[:, None] == jnp.arange(mode_table.shape[0], dtype=jnp.int32)[None, :]
    ).astype(F32)
    panel_hits = (panels[:, None] == jnp.arange(NP, dtype=jnp.int32)[None, :]).astype(F32)
    summed = jnp.dot(panel_hits.T, shape_hits * load[:, None], precision=lax.Precision.HIGHEST)
    partial_forces = jnp.dot(summed, mode_table, precision=lax.Precision.HIGHEST)
    owned = NP // count
    blocks = lax.all_to_all(
        partial_forces.reshape(count, owned, -1), "gx", split_axis=0, concat_axis=0, tiled=True
    )
    spans = lax.axis_size("gz")
    mine = jnp.broadcast_to(jnp.sum(blocks, axis=0)[None], (spans, owned, mode_table.shape[1]))
    forces = jnp.sum(lax.all_to_all(mine, "gz", split_axis=0, concat_axis=0, tiled=True), axis=0)
    return (
        new_density.reshape(density.shape),
        new_momentum.reshape(momentum.shape),
        new_energy.reshape(energy.shape),
        forces,
    )


def solution(mesh):
    in_specs = (
        P("gx", "gz", None),
        P(None, "gx", "gz", None),
        P("gx", "gz", None),
        P("gx", "gz", None),
        P(),
        P(),
        P("gx", "gz"),
        P("gx", "gz"),
        P(),
    )
    out_specs = (P("gx", "gz", None), P(None, "gx", "gz", None), P("gx", "gz", None), P("gx", None))
    return jax.shard_map(body, mesh=mesh, in_specs=in_specs, out_specs=out_specs, check_vma=False)
```

time: 807 us -> 440 us (0.55); the launches traced: 797 us -> 439 us
  blocking collectives: 281 us -> 9.65 us
  Pallas kernels: 0 us -> 139 us
  local copies, waits for them, and re-layouts: 148 us -> 10.4 us
  matrix products: 80.9 us -> 2.16 us
  other arithmetic: 71.7 us -> 1.29 us
  waiting for transfers between devices: 198 us -> 250 us
  starting transfers between devices: 16 us -> 25.3 us
    all_to_all x2 -> x1, blocking collectives: 242 us -> 9.65 us  [body(): lax.all_to_all(partial_forces.reshape(count, owned, -1), 'gx', split_axis...]
    pallas_call x0 -> x7, Pallas kernels: none -> 139 us  [the longest x2 57.5 us: x_terms(): pl.pallas_call(matmul_kernel, out_shape=jax.ShapeDtypeStruct((FIELDS, len...]
    dot_general x4 -> x0, matrix products: 78.8 us -> none  [the longest x2 39.5 us: x_terms(): jnp.einsum('ij,kjzy->kizy', deriv_matrix, flux, precision=lax.Precision.H...]
    all_to_all x2 -> x3, waiting for transfers between devices: 198 us -> 250 us  [the longest x1 135 us: body(): lax.all_to_all(packed, 'gx', split_axis=0, concat_axis=0, tiled=True)]
    all_to_all x6 -> x0, local copies, waits for them, and re-layouts: 47.8 us -> none  [the longest x4 25.7 us: rate(): lax.all_to_all(state, 'gx', split_axis=2, concat_axis=1, tiled=True)]
    add x2 -> x0, other arithmetic: 41.1 us -> none  [the longest x1 20.8 us: body(): 0.5 * state]
    psum x1 -> x0, blocking collectives: 39.4 us -> none  [body(): everything = lax.psum(partial_forces, ('gx', 'gz'))]
    unnamed x73 -> x28, local copies, waits for them, and re-layouts: 29.9 us -> 3.11 us
  transfers between devices with their start and end apart: 6 -> 11, of which waited for: 2 -> 2; matrix products, arithmetic and copies ran while one was open for 5% -> 0% of each run, Pallas kernels for 0% -> 16%
where the time goes in v1:
time: 440 us; the launch traced here: 439 us
  waiting for transfers between devices  250 us (57%)
  Pallas kernels  139 us (32%)
  starting transfers between devices  25.3 us (6%)
  local copies, waits for them, and re-layouts  10.4 us (2%)
  blocking collectives  9.65 us (2%)
    all_to_all x1, waiting for transfers between devices, body(): lax.all_to_all(packed, 'gx', split_axis=0, concat_axis=0, tiled=True)  135 us
    all_to_all x1, waiting for transfers between devices, body(): back = lax.all_to_all(final, 'gx', split_axis=0, concat_axis=0, tiled=True)  114 us
    pallas_call x2, Pallas kernels, x_terms(): pl.pallas_call(matmul_kernel, out_shape=jax.ShapeDtypeStruct((FIELDS, len...  57.5 us
    pallas_call x1, Pallas kernels, body(): pl.pallas_call(functools.partial(finish_kernel, False), out_shape=(jax.Sh...  21.3 us
    pallas_call x1, Pallas kernels, body(): pl.pallas_call(functools.partial(pack_kernel, count, z_cells, order), out...  18.4 us
    pallas_call x1, Pallas kernels, body(): pl.pallas_call(functools.partial(finish_kernel, True), out_shape=jax.Shap...  16.4 us
    pallas_call x1, Pallas kernels, body(): pl.pallas_call(functools.partial(unpack_kernel, count, z_cells, order), o...  14.4 us
    pallas_call x1, Pallas kernels, body(): pl.pallas_call(edge_kernel, out_shape=edge_shape, in_specs=whole(2), out_...  10.6 us
  transfers between devices with their start and end apart: 11, of which 2 were waited for; matrix products, arithmetic and copies ran while one was open for 0% of the time, Pallas kernels for 16%

profile of v1, /device:TPU:1, one launch (start us, length us, event | category | flops | bytes accessed | tf_op | source)
XLA Modules:
  0.0 439.2 jit_solution(9170779728994373940)
XLA Ops:
  0.6 18.4 %shard_map.147 = f32[8,6,128,256]{3,2,1,0:T(8,128)} custom-call(f32[2048,128]{1,0:T(8,128)} %bitcast.39, f32[3,2048,128]{2,1,0:T(8,128)} %bitcast.38, f32[2048,128]{1,0:T(8,128)} %bitcast.40, f32[2048,128]{1,0:T(8,128)} %bitcast.37), custom_call_target="tpu_custom_call" | custom-call | tf_op jit(solution)/shard_map/pallas_call | solution.py:335
  19.0 6.5 %all-to-all-start = ((f32[8,6,128,256]{3,2,1,0:T(8,128)}), f32[8,6,128,256]{3,2,1,0:T(8,128)}, u32[]{:S(2)}, u32[]{:S(2)}) async-start(f32[8,6,128,256]{3,2,1,0:T(8,128)} %shard_map.147), calls=%async_computation | async-start | bytes 12582912 | tf_op jit(solution)/shard_map/all_to_all | solution.py:342
  25.5 0.7 compare_reduce_fusion
  27.5 135.4 %all-to-all-done.q.refs_0_ = f32[8,6,128,256]{3,2,1,0:T(8,128)} async-done(((f32[8,6,128,256]{3,2,1,0:T(8,128)}), f32[8,6,128,256]{3,2,1,0:T(8,128)}, u32[]{:S(2)}, u32[]{:S(2)}) %all-to-all-start) | async-done | bytes 6291488 | tf_op jit(solution)/shard_map/all_to_all | solution.py:342
  162.9 10.6 %shard_map.149 = f32[4,5,256,128]{3,2,1,0:T(8,128)} custom-call(f32[8,6,128,256]{3,2,1,0:T(8,128)} %all-to-all-done.q.refs_0_, bf16[256,128]{1,0:T(8,128)(2,1)} %constant.37.clone.select.refs_8_), custom_call_target="tpu_custom_call" | custom-call | tf_op jit(solution)/shard_map/pallas_call | solution.py:363
  173.5 1.9 slice_bitcast_fusion
  175.4 0.6 collective-permute-start
  176.0 1.1 collective-permute-start.1
  177.1 3.3 collective-permute-start.2
  180.4 28.9 %shard_map.148.refs_1_ = f32[5,1024,256]{2,1,0:T(8,128)} custom-call(f32[8,6,128,256]{3,2,1,0:T(8,128)} %all-to-all-done.q.refs_0_, f32[1024,1024]{1,0:T(8,128)} %deriv.3, f32[1024,1024]{1,0:T(8,128)} %smooth.3), custom_call_target="tpu_custom_call" | custom-call | flops 16106127360 | bytes 52428800 | tf_op jit(solution)/shard_map/pallas_call | solution.py:345
  209.4 0.7 iota.26.refs_6_.refs_7_
  210.4 0.2 copy-done.6
  210.6 0.2 copy-done.8
  210.8 21.3 %shard_map.150 = (f32[8,5,128,256]{3,2,1,0:T(8,128)}, f32[4,5,256,128]{3,2,1,0:T(8,128)}) custom-call(f32[8,6,128,256]{3,2,1,0:T(8,128)} %all-to-all-done.q.refs_0_, f32[5,1024,256]{2,1,0:T(8,128)} %shard_map.148.refs_1_, f32[5,256,128]{2,1,0:T(8,128)} %copy-done.2, f32[5,256,128]{2,1,0:T(8,128)} %copy-done.4, f32[5,256,128]{2,1,0:T(8,128)} %copy-done.6, ...), custom_call_target="tpu_custom_call" | custom-call | tf_op jit(solution)/shard_map/pallas_call | solution.py:372
  232.2 1.9 slice_bitcast_fusion.4
  234.2 1.5 collective-permute-start.5
  235.6 2.3 collective-permute-start.6
  237.9 28.6 %shard_map.151.refs_2_ = f32[5,1024,256]{2,1,0:T(8,128)} custom-call(f32[8,5,128,256]{3,2,1,0:T(8,128)} %get-tuple-element.11.q.refs_1_, f32[1024,1024]{1,0:T(8,128)} %deriv.3, f32[1024,1024]{1,0:T(8,128)} %smooth.3), custom_call_target="tpu_custom_call" | custom-call | flops 16106127360 | bytes 52428800 | tf_op jit(solution)/shard_map/pallas_call | solution.py:345
  266.6 0.8 copy-done.3
  267.8 0.9 copy-done.9
  268.7 16.4 %shard_map.152 = f32[8,5,128,256]{3,2,1,0:T(8,128)} custom-call(f32[8,6,128,256]{3,2,1,0:T(8,128)} %all-to-all-done.q.refs_0_, f32[8,5,128,256]{3,2,1,0:T(8,128)} %get-tuple-element.11.q.refs_1_, f32[5,1024,256]{2,1,0:T(8,128)} %shard_map.151.refs_2_, f32[5,256,128]{2,1,0:T(8,128)} %copy-done.3, f32[5,256,128]{2,1,0:T(8,128)} %copy-done.5, ...), custom_call_target="tpu_custom_call" | custom-call | tf_op jit(solution)/shard_map/pallas_call | solution.py:381
  285.1 4.8 %all-to-all-start.1 = ((f32[8,5,128,256]{3,2,1,0:T(8,128)}), f32[8,5,128,256]{3,2,1,0:T(8,128)}, u32[]{:S(2)}, u32[]{:S(2)}) async-start(f32[8,5,128,256]{3,2,1,0:T(8,128)} %shard_map.152), calls=%async_computation.1 | async-start | bytes 10485760 | tf_op jit(solution)/shard_map/all_to_all | solution.py:389
  289.9 0.3 slice_reduce_fusion
  290.7 114.3 %all-to-all-done.1.packed = f32[8,5,128,256]{3,2,1,0:T(8,128)} async-done(((f32[8,5,128,256]{3,2,1,0:T(8,128)}), f32[8,5,128,256]{3,2,1,0:T(8,128)}, u32[]{:S(2)}, u32[]{:S(2)}) %all-to-all-start.1) | async-done | bytes 5242912 | tf_op jit(solution)/shard_map/all_to_all | solution.py:389
  405.0 1.1 slice.78
  406.1 0.2 copy.26
  406.6 1.9 fusion
  408.8 9.7 %all_to_all.20 = f32[8,8,128]{2,1,0:T(8,128)S(1)} all-to-all(f32[8,8,128]{2,1,0:T(8,128)S(1)} %convolution_bitcast_fusion), channel_id=1, replica_groups=mesh['gx'=8,'gz'=4] {'gx'}, dimensions={0} | all-to-all | bytes 65536 | tf_op jit(solution)/shard_map/all_to_all | solution.py:413
  418.5 0.6 broadcast_in_dim.18
  419.1 5.1 %all-to-all-start.3 = ((f32[4,8,128]{2,1,0:T(8,128)}), f32[4,8,128]{2,1,0:T(8,128)S(1)}, u32[]{:S(2)}, u32[]{:S(2)}) async-start(f32[4,8,128]{2,1,0:T(8,128)} %broadcast_in_dim.18), calls=%async_computation.3 | async-start | bytes 32768 | tf_op jit(solution)/shard_map/all_to_all | solution.py:418
  424.2 14.4 %shard_map.153 = (f32[2048,128]{1,0:T(8,128)}, f32[3,2048,128]{2,1,0:T(8,128)}, f32[2048,128]{1,0:T(8,128)}) custom-call(f32[8,5,128,256]{3,2,1,0:T(8,128)} %all-to-all-done.1.packed), custom_call_target="tpu_custom_call" | custom-call | tf_op jit(solution)/shard_map/pallas_call | solution.py:390
  438.6 0.6 reduce_sum.19
  (47 shorter events, 1.8 us)
Async XLA Ops:
  0.6 407.9 %copy-start = (f32[256,128]{1,0:T(8,128)S(1)}, f32[256,128]{1,0:T(8,128)}, u32[]{:S(2)}) copy-start(f32[256,128]{1,0:T(8,128)} %param.20) | copy-start | bytes 393220
  19.0 6.5 %copy-start.12 = (s32[8]{0:T(128)S(1)}, s32[8]{0:T(128)}, u32[]{:S(2)}) copy-start(s32[8]{0:T(128)} %constant.39.clone) | copy-start | bytes 100
  19.0 143.9 %all-to-all-start = ((f32[8,6,128,256]{3,2,1,0:T(8,128)}), f32[8,6,128,256]{3,2,1,0:T(8,128)}, u32[]{:S(2)}, u32[]{:S(2)}) async-start(f32[8,6,128,256]{3,2,1,0:T(8,128)} %shard_map.147), calls=%async_computation | async-start | bytes 12582912 | tf_op jit(solution)/shard_map/all_to_all | solution.py:342
  175.4 33.9 %collective-permute-start = (f32[5,256,128]{2,1,0:T(8,128)S(1)}, f32[5,256,128]{2,1,0:T(8,128)S(1)}, u32[]{:S(2)}, u32[]{:S(2)}) collective-permute-start(f32[5,256,128]{2,1,0:T(8,128)S(1)} %get-tuple-element.23), channel_id=1, source_target_pairs={{0,8},{8,16},{16,24},{24,28},{28,20},{20,12},{12,4},{4,0},{1,9},{9... | collective-permute-start | bytes 1966088 | tf_op jit(solution)/shard_map/ppermute | solution.py:304
  176.0 33.3 %collective-permute-start.1 = (f32[5,256,128]{2,1,0:T(8,128)S(1)}, f32[5,256,128]{2,1,0:T(8,128)S(1)}, u32[]{:S(2)}, u32[]{:S(2)}) collective-permute-start(f32[5,256,128]{2,1,0:T(8,128)S(1)} %get-tuple-element.22), channel_id=1, source_target_pairs={{0,4},{8,0},{16,8},{24,16},{28,24},{20,28},{12,20},{4,12},{1,5},{9... | collective-permute-start | bytes 1966088 | tf_op jit(solution)/shard_map/ppermute | solution.py:305
  177.1 32.2 %collective-permute-start.2 = (f32[5,256,128]{2,1,0:T(8,128)S(1)}, f32[5,256,128]{2,1,0:T(8,128)S(1)}, u32[]{:S(2)}, u32[]{:S(2)}) collective-permute-start(f32[5,256,128]{2,1,0:T(8,128)S(1)} %get-tuple-element.21), channel_id=1, source_target_pairs={{0,1},{1,2},{2,3},{3,0},{4,5},{5,6},{6,7},{7,4},{8,9},{9,10},{10,1... | collective-permute-start | bytes 1966088 | tf_op jit(solution)/shard_map/ppermute | solution.py:306
  180.4 28.9 %collective-permute-start.3 = (f32[5,256,128]{2,1,0:T(8,128)S(1)}, f32[5,256,128]{2,1,0:T(8,128)S(1)}, u32[]{:S(2)}, u32[]{:S(2)}) collective-permute-start(f32[5,256,128]{2,1,0:T(8,128)S(1)} %get-tuple-element.20), channel_id=1, source_target_pairs={{0,3},{1,0},{2,1},{3,2},{4,7},{5,4},{6,5},{7,6},{8,11},{9,8},{10,9... | collective-permute-start | bytes 1966088 | tf_op jit(solution)/shard_map/ppermute | solution.py:307
  209.3 0.8 copy-start.2
  209.3 1.0 copy-start.4
  209.3 1.3 copy-start.6
  209.4 1.5 copy-start.8
  234.1 32.4 %collective-permute-start.4 = (f32[5,256,128]{2,1,0:T(8,128)S(1)}, f32[5,256,128]{2,1,0:T(8,128)S(1)}, u32[]{:S(2)}, u32[]{:S(2)}) collective-permute-start(f32[5,256,128]{2,1,0:T(8,128)S(1)} %get-tuple-element.19), channel_id=1, source_target_pairs={{0,8},{8,16},{16,24},{24,28},{28,20},{20,12},{12,4},{4,0},{1,9},{9... | collective-permute-start | bytes 1966088 | tf_op jit(solution)/shard_map/ppermute | solution.py:304
  234.2 32.4 %collective-permute-start.5 = (f32[5,256,128]{2,1,0:T(8,128)S(1)}, f32[5,256,128]{2,1,0:T(8,128)S(1)}, u32[]{:S(2)}, u32[]{:S(2)}) collective-permute-start(f32[5,256,128]{2,1,0:T(8,128)S(1)} %get-tuple-element.18), channel_id=1, source_target_pairs={{0,4},{8,0},{16,8},{24,16},{28,24},{20,28},{12,20},{4,12},{1,5},{9... | collective-permute-start | bytes 1966088 | tf_op jit(solution)/shard_map/ppermute | solution.py:305
  235.6 30.9 %collective-permute-start.6 = (f32[5,256,128]{2,1,0:T(8,128)S(1)}, f32[5,256,128]{2,1,0:T(8,128)S(1)}, u32[]{:S(2)}, u32[]{:S(2)}) collective-permute-start(f32[5,256,128]{2,1,0:T(8,128)S(1)} %get-tuple-element.17), channel_id=1, source_target_pairs={{0,1},{1,2},{2,3},{3,0},{4,5},{5,6},{6,7},{7,4},{8,9},{9,10},{10,1... | collective-permute-start | bytes 1966088 | tf_op jit(solution)/shard_map/ppermute | solution.py:306
  237.9 28.6 %collective-permute-start.7 = (f32[5,256,128]{2,1,0:T(8,128)S(1)}, f32[5,256,128]{2,1,0:T(8,128)S(1)}, u32[]{:S(2)}, u32[]{:S(2)}) collective-permute-start(f32[5,256,128]{2,1,0:T(8,128)S(1)} %get-tuple-element.16), channel_id=1, source_target_pairs={{0,3},{1,0},{2,1},{3,2},{4,7},{5,4},{6,5},{7,6},{8,11},{9,8},{10,9... | collective-permute-start | bytes 1966088 | tf_op jit(solution)/shard_map/ppermute | solution.py:307
  266.5 0.8 copy-start.3
  266.5 1.0 copy-start.5
  266.5 1.2 copy-start.7
  267.8 0.9 copy-start.9
  285.1 4.8 %copy-start.1 = (f32[128,16,128]{2,1,0:T(8,128)S(1)}, f32[128,16,128]{2,1,0:T(8,128)}, u32[]{:S(2)}) copy-start(f32[128,16,128]{2,1,0:T(8,128)} %param.15) | copy-start | bytes 3145732
  285.1 5.2 %copy-start.10 = (s32[128,16]{0,1:T(8,128)S(1)}, s32[128,16]{0,1:T(8,128)}, u32[]{:S(2)}) copy-start(s32[128,16]{0,1:T(8,128)} %param.18) | copy-start | bytes 24580
  285.1 5.4 %copy-start.11 = (s32[128,16]{0,1:T(8,128)S(1)}, s32[128,16]{0,1:T(8,128)}, u32[]{:S(2)}) copy-start(s32[128,16]{0,1:T(8,128)} %param.19) | copy-start | bytes 24580
  285.1 119.9 %all-to-all-start.1 = ((f32[8,5,128,256]{3,2,1,0:T(8,128)}), f32[8,5,128,256]{3,2,1,0:T(8,128)}, u32[]{:S(2)}, u32[]{:S(2)}) async-start(f32[8,5,128,256]{3,2,1,0:T(8,128)} %shard_map.152), calls=%async_computation.1 | async-start | bytes 10485760 | tf_op jit(solution)/shard_map/all_to_all | solution.py:389
  419.1 19.5 %all-to-all-start.3 = ((f32[4,8,128]{2,1,0:T(8,128)}), f32[4,8,128]{2,1,0:T(8,128)S(1)}, u32[]{:S(2)}, u32[]{:S(2)}) async-start(f32[4,8,128]{2,1,0:T(8,128)} %broadcast_in_dim.18), calls=%async_computation.3 | async-start | bytes 32768 | tf_op jit(solution)/shard_map/all_to_all | solution.py:418

commit v2 on v1

--- a/solution.py
+++ b/solution.py
@@ -92,10 +92,14 @@
     return rows
 
 
-def pack_kernel(count, z_cells, order, density, momentum, energy, metric, out):
+def pack_kernel(count, z_cells, order, *refs):
+    out = refs[-1]
     x_cells = out.shape[2]
     width = LANES // count
-    sources = [density, momentum.at[0], momentum.at[1], momentum.at[2], energy, metric]
+    sources = refs[:-1]
+    if len(sources) == 3:
+        density, momentum, energy = sources
+        sources = [density, momentum.at[0], momentum.at[1], momentum.at[2], energy]
 
     @pl.loop(0, x_cells // 8)
     def _(chunk):
@@ -110,7 +114,13 @@
                     out[order[t], field, pl.ds(row, 8), half * LANES : (half + 1) * LANES] = tiles[t]
 
 
-def unpack_kernel(count, z_cells, order, packed, density, momentum, energy):
+def unpack_kernel(count, z_cells, order, *refs):
+    parts, (density, momentum, energy) = refs[:-3], refs[-3:]
+    for half, packed in enumerate(parts):
+        unpack_part(count, z_cells, order, half * packed.shape[2], packed, density, momentum, energy)
+
+
+def unpack_part(count, z_cells, order, first_row, packed, density, momentum, energy):
     x_cells = packed.shape[2]
     width = LANES // count
     targets = [density, momentum.at[0], momentum.at[1], momentum.at[2], energy]
@@ -125,18 +135,20 @@
                 ]
                 planes = swap_groups(tiles, width)
                 for k in range(count):
-                    target[pl.ds(row * z_cells + half * count + k, 8, stride=z_cells), :] = planes[k]
-
-
-def matmul_kernel(q, deriv, smooth, out, left_high, left_low, right_high, right_low):
+                    target[pl.ds((first_row + row) * z_cells + half * count + k, 8, stride=z_cells), :] = planes[k]
+
+
+def matmul_kernel(half, parts, q, deriv, smooth, out, left_high, left_low, right_high, right_low):
     blocks, _, x_cells, lanes = q.shape
     length = blocks * x_cells
-
-    @pl.loop(0, length // 32)
+    span = x_cells // parts
+
+    @pl.loop(0, length // parts // 32)
     def _(chunk):
         row = pl.multiple_of(chunk * 32, 32)
+        source = pl.multiple_of(row // span * x_cells + half * span + row % span, 32)
         for column, matrix, sign in ((0, smooth, 1.0), (1, deriv, -1.0)):
-            high, low = split2(sign * matrix[pl.ds(row, 32), :])
+            high, low = split2(sign * matrix[pl.ds(source, 32), :])
             left_high[pl.ds(row, 32), column * length : (column + 1) * length] = high
             left_low[pl.ds(row, 32), column * length : (column + 1) * length] = low
 
@@ -155,9 +167,9 @@
                     right_high[f, at, :] = high
                     right_low[f, at, :] = low
 
-    tall = min(512, length)
-
-    @pl.loop(0, length // tall)
+    tall = min(512, length // parts)
+
+    @pl.loop(0, length // parts // tall)
     def _(part):
         row = pl.multiple_of(part * tall, tall)
 
@@ -195,20 +207,23 @@
                 out[d, f, pl.ds(row, step), :] = value
 
 
-def finish_kernel(second, *refs):
+def finish_kernel(second, half, parts, *refs):
     if second:
-        start, q, x_part, h0, h1, h2, h3, mask, weights, out, high, low = refs
+        start, metric, q, x_part, h0, h1, h2, h3, mask, weights, out, high, low = refs
         edges_out = None
     else:
-        q, x_part, h0, h1, h2, h3, mask, weights, select, out, edges_out, high, low, made = refs
+        q, metric, x_part, h0, h1, h2, h3, mask, weights, select, out, edges_out, high, low, made = refs
         start = q
     blocks, _, x_cells, lanes = q.shape
     step = 32
-    quarter_rows = blocks * x_cells // 4
+    span = x_cells // parts
+    quarter_rows = blocks * span // 4
 
     @pl.loop(0, quarter_rows // step)
     def _(chunk):
-        row = pl.multiple_of(chunk * step, step)
+        here = pl.multiple_of(chunk * step, step)
+        row = pl.multiple_of(here // span * x_cells + half * span + here % span, step)
+        kept = pl.multiple_of(here % span, step)
         halo = []
         for f in range(FIELDS):
             halo.append(swap_groups([h[f, pl.ds(row, step), :] for h in (h0, h1, h2, h3)], EDGE))
@@ -237,8 +252,8 @@
         slopes += jnp.dot(low[...], weights[...], preferred_element_type=F32)
         for quarter in range(4):
             block, at = rows_of(quarter, row, blocks, x_cells)
-            scale = time_step * start[block, FIELDS, pl.ds(at, step), :]
-            whole_row = pl.ds(pl.multiple_of(quarter * quarter_rows + row, step), step)
+            scale = time_step * metric[block, 0, pl.ds(at, step), :]
+            whole_row = pl.ds(pl.multiple_of(quarter * quarter_rows + here, step), step)
             for f in range(FIELDS):
                 base = (quarter * FIELDS + f) * step
                 total = x_part[f, whole_row, :] - slopes[base : base + step, :] * (1.0 / 12.0)
@@ -247,7 +262,7 @@
                     value = 0.5 * start[block, f, pl.ds(at, step), :] + 0.5 * value
                 else:
                     made[base : base + step, :] = value
-                out[block, f, pl.ds(at, step), :] = value
+                out[block, f, pl.ds(kept, step), :] = value
         if not second:
             edges = edges_of(made[...], select[...])
             for f in range(FIELDS):
@@ -332,25 +347,32 @@
     flat = (x_cells * z_cells, y_cells)
     select, weights = tables(z_cells, tile_y)
 
-    packed = pl.pallas_call(
-        functools.partial(pack_kernel, count, z_cells, order),
-        out_shape=jax.ShapeDtypeStruct((count, FIELDS + 1, x_cells, lanes), F32),
-        in_specs=whole(4),
-        out_specs=whole(1)[0],
-        compiler_params=params(),
-    )(density.reshape(flat), momentum.reshape((3,) + flat), energy.reshape(flat), metric.reshape(flat))
-    start = lax.all_to_all(packed, "gx", split_axis=0, concat_axis=0, tiled=True)
-
-    def x_terms(state):
+    def pack(fields, *arrays):
         return pl.pallas_call(
-            matmul_kernel,
-            out_shape=jax.ShapeDtypeStruct((FIELDS, length, lanes), F32),
+            functools.partial(pack_kernel, count, z_cells, order),
+            out_shape=jax.ShapeDtypeStruct((count, fields, x_cells, lanes), F32),
+            in_specs=whole(len(arrays)),
+            out_specs=whole(1)[0],
+            compiler_params=params(),
+        )(*arrays)
+
+    def swap(array):
+        return lax.all_to_all(array, "gx", split_axis=0, concat_axis=0, tiled=True)
+
+    start = swap(pack(FIELDS, density.reshape(flat), momentum.reshape((3,) + flat), energy.reshape(flat)))
+    packed_metric, start = lax.optimization_barrier((pack(1, metric.reshape(flat)), start))
+    tile_metric = swap(packed_metric)
+
+    def x_terms(state, half, parts):
+        return pl.pallas_call(
+            functools.partial(matmul_kernel, half, parts),
+            out_shape=jax.ShapeDtypeStruct((FIELDS, length // parts, lanes), F32),
             in_specs=whole(3),
             out_specs=whole(1)[0],
-            scratch_shapes=[pltpu.VMEM((length, 2 * length), BF16)] * 2
+            scratch_shapes=[pltpu.VMEM((length // parts, 2 * length), BF16)] * 2
             + [pltpu.VMEM((FIELDS, 2 * length, lanes), BF16)] * 2,
             compiler_params=params(),
-            cost_estimate=cost(12 * FIELDS * length * length * lanes, 40 * FIELDS * length * lanes),
+            cost_estimate=cost(12 * FIELDS * length * length * lanes // parts, 40 * FIELDS * length * lanes),
         )(state, deriv_matrix, smooth_matrix)
 
     edge_shape = jax.ShapeDtypeStruct((4, FIELDS, length // 4, LANES), F32)
@@ -370,23 +392,27 @@
     halo = exchange(edges, order)
     split_rows = [pltpu.VMEM((4 * FIELDS * 32, 2 * lanes + LANES), BF16)] * 2
     first, edges = pl.pallas_call(
-        functools.partial(finish_kernel, False),
+        functools.partial(finish_kernel, False, 0, 1),
         out_shape=(jax.ShapeDtypeStruct((count, FIELDS, x_cells, lanes), F32), edge_shape),
-        in_specs=whole(9),
+        in_specs=whole(10),
         out_specs=tuple(whole(2)),
         scratch_shapes=split_rows + [pltpu.VMEM((4 * FIELDS * 32, lanes), F32)],
         compiler_params=params(),
-    )(start, x_terms(start), *halo, mask, weights, select)
+    )(start, tile_metric, x_terms(start, 0, 1), *halo, mask, weights, select)
     halo = exchange(edges, order)
-    final = pl.pallas_call(
-        functools.partial(finish_kernel, True),
-        out_shape=jax.ShapeDtypeStruct((count, FIELDS, x_cells, lanes), F32),
-        in_specs=whole(9),
-        out_specs=whole(1)[0],
-        scratch_shapes=split_rows,
-        compiler_params=params(),
-    )(start, first, x_terms(first), *halo, mask, weights)
-    back = lax.all_to_all(final, "gx", split_axis=0, concat_axis=0, tiled=True)
+    back, parts = [], 1
+    for half in range(parts):
+        final = pl.pallas_call(
+            functools.partial(finish_kernel, True, half, parts),
+            out_shape=jax.ShapeDtypeStruct((count, FIELDS, x_cells // parts, lanes), F32),
+            in_specs=whole(10),
+            out_specs=whole(1)[0],
+            scratch_shapes=split_rows,
+            compiler_params=params(),
+            cost_estimate=cost(10**10, 40 * FIELDS * length * lanes // parts),
+        )(start, tile_metric, first, x_terms(first, half, parts), *halo, mask, weights)
+        final, first = lax.optimization_barrier((final, first))
+        back.append(swap(final))
     new_density, new_momentum, new_energy = pl.pallas_call(
         functools.partial(unpack_kernel, count, z_cells, order),
         out_shape=(
@@ -394,12 +420,12 @@
             jax.ShapeDtypeStruct((3,) + flat, F32),
             jax.ShapeDtypeStruct(flat, F32),
         ),
-        in_specs=whole(1),
+        in_specs=whole(parts),
         out_specs=tuple(whole(3)),
         compiler_params=params(),
-    )(back)
-
-    floor = back[order[0]].reshape(FIELDS, x_cells, z_cells, tile_y)[..., 0]
+    )(*back)
+
+    floor = jnp.concatenate([part[order[0]] for part in back], axis=1).reshape(FIELDS, x_cells, z_cells, tile_y)[..., 0]
     load = ((pressure_of(floor) - pressure_ref) * metric[:, :, 0]).reshape(-1)
     panels = panel_of_cell.reshape(-1)
     shapes = shape_index.reshape(-1)

time: 440 us -> 417 us (0.948)
  waiting for transfers between devices: 250 us -> 221 us
  starting transfers between devices: 25.3 us -> 30 us
    all_to_all x2 -> x3, waiting for transfers between devices: 250 us -> 221 us  [swap(): return lax.all_to_all(array, 'gx', split_axis=0, concat_axis=0, tiled=True)]
    all_to_all x2 -> x3, starting transfers between devices: 11.3 us -> 17 us  [swap(): return lax.all_to_all(array, 'gx', split_axis=0, concat_axis=0, tiled=True)]
    pallas_call x5 -> x6, Pallas kernels: 114 us -> 114 us  [the longest x2 57.6 us: x_terms(): pl.pallas_call(functools.partial(matmul_kernel, half, parts), out_shape=j...]
  transfers between devices with their start and end apart: 11 -> 12, of which waited for: 2 -> 2; matrix products, arithmetic and copies ran while one was open for 0% -> 1% of each run, Pallas kernels for 16% -> 21%
where the time goes in v2:
time: 417 us; the launch traced here: 416 us
  waiting for transfers between devices  221 us (53%)
  Pallas kernels  139 us (33%)
  starting transfers between devices  30 us (7%)
  local copies, waits for them, and re-layouts  10.5 us (3%)
  blocking collectives  9.99 us (2%)
    all_to_all x3, waiting for transfers between devices, swap(): return lax.all_to_all(array, 'gx', split_axis=0, concat_axis=0, tiled=True)  221 us
    pallas_call x2, Pallas kernels, x_terms(): pl.pallas_call(functools.partial(matmul_kernel, half, parts), out_shape=j...  57.6 us
    pallas_call x1, Pallas kernels, body(): pl.pallas_call(functools.partial(finish_kernel, False, 0, 1), out_shape=(...  21.3 us
    pallas_call x2, Pallas kernels, pack(): pl.pallas_call(functools.partial(pack_kernel, count, z_cells, order), out...  18.8 us
    all_to_all x3, starting transfers between devices, swap(): return lax.all_to_all(array, 'gx', split_axis=0, concat_axis=0, tiled=True)  17 us
    pallas_call x1, Pallas kernels, body(): pl.pallas_call(functools.partial(finish_kernel, True, half, parts), out_s...  16.6 us
    pallas_call x1, Pallas kernels, body(): pl.pallas_call(functools.partial(unpack_kernel, count, z_cells, order), o...  14.4 us
    pallas_call x1, Pallas kernels, body(): pl.pallas_call(edge_kernel, out_shape=edge_shape, in_specs=whole(2), out_...  10.3 us
  transfers between devices with their start and end apart: 12, of which 2 were waited for; matrix products, arithmetic and copies ran while one was open for 1% of the time, Pallas kernels for 21%

profile of v2, /device:TPU:1, one launch (start us, length us, event | category | flops | bytes accessed | tf_op | source)
XLA Modules:
  0.0 416.2 jit_solution(12671031598429551113)
XLA Ops:
  0.6 13.0 %shard_map.148 = f32[8,5,128,256]{3,2,1,0:T(8,128)} custom-call(f32[2048,128]{1,0:T(8,128)} %bitcast.39, f32[3,2048,128]{2,1,0:T(8,128)} %bitcast.38, f32[2048,128]{1,0:T(8,128)} %bitcast.40), custom_call_target="tpu_custom_call" | custom-call | tf_op jit(solution)/shard_map/pallas_call | solution.py:351
  13.6 6.5 %all-to-all-start = ((f32[8,5,128,256]{3,2,1,0:T(8,128)}), f32[8,5,128,256]{3,2,1,0:T(8,128)}, u32[]{:S(2)}, u32[]{:S(2)}) async-start(f32[8,5,128,256]{3,2,1,0:T(8,128)} %shard_map.148), calls=%async_computation | async-start | bytes 10485760 | tf_op jit(solution)/shard_map/all_to_all | solution.py:360
  20.1 5.9 %shard_map.147 = f32[8,1,128,256]{3,2,1,0:T(8,128)} custom-call(f32[2048,128]{1,0:T(8,128)} %bitcast.37), custom_call_target="tpu_custom_call" | custom-call | tf_op jit(solution)/shard_map/pallas_call | solution.py:351
  26.0 0.7 compare_reduce_fusion
  27.9 107.1 %all-to-all-done.q.refs_0_ = f32[8,5,128,256]{3,2,1,0:T(8,128)} async-done(((f32[8,5,128,256]{3,2,1,0:T(8,128)}), f32[8,5,128,256]{3,2,1,0:T(8,128)}, u32[]{:S(2)}, u32[]{:S(2)}) %all-to-all-start) | async-done | bytes 5242912 | tf_op jit(solution)/shard_map/all_to_all | solution.py:360
  135.0 4.7 %all-to-all-start.1 = ((f32[8,1,128,256]{3,2,1,0:T(8,128)}), f32[8,1,128,256]{3,2,1,0:T(8,128)S(1)}, u32[]{:S(2)}, u32[]{:S(2)}) async-start(f32[8,1,128,256]{3,2,1,0:T(8,128)} %shard_map.147), calls=%async_computation.1 | async-start | bytes 2097152 | tf_op jit(solution)/shard_map/all_to_all | solution.py:360
  139.7 10.3 %shard_map.150 = f32[4,5,256,128]{3,2,1,0:T(8,128)} custom-call(f32[8,5,128,256]{3,2,1,0:T(8,128)} %all-to-all-done.q.refs_0_, bf16[256,128]{1,0:T(8,128)(2,1)} %constant.37.clone.select.refs_9_), custom_call_target="tpu_custom_call" | custom-call | tf_op jit(solution)/shard_map/pallas_call | solution.py:385
  150.0 1.9 slice_bitcast_fusion
  152.0 1.5 collective-permute-start
  153.5 2.4 collective-permute-start.2
  156.0 28.9 %shard_map.149.refs_2_ = f32[5,1024,256]{2,1,0:T(8,128)} custom-call(f32[8,5,128,256]{3,2,1,0:T(8,128)} %all-to-all-done.q.refs_0_, f32[1024,1024]{1,0:T(8,128)} %deriv.3, f32[1024,1024]{1,0:T(8,128)} %smooth.3), custom_call_target="tpu_custom_call" | custom-call | flops 16106127360 | bytes 52428800 | tf_op jit(solution)/shard_map/pallas_call | solution.py:367
  184.9 0.7 iota.26.refs_7_.refs_8_
  185.9 0.2 copy-done.5
  186.1 0.3 copy-done.2
  186.5 21.3 %shard_map.151 = (f32[8,5,128,256]{3,2,1,0:T(8,128)}, f32[4,5,256,128]{3,2,1,0:T(8,128)}) custom-call(f32[8,5,128,256]{3,2,1,0:T(8,128)} %all-to-all-done.q.refs_0_, f32[8,1,128,256]{3,2,1,0:T(8,128)} %copy-done.2, f32[5,1024,256]{2,1,0:T(8,128)} %shard_map.149.refs_2_, f32[5,256,128]{2,1,0:T(8,128)} %copy-done.3, f32[5,256,128]{2,1,0:T(8,128)} %copy-done.4, ...), custom_call_target="tpu_custom_call" | custom-call | tf_op jit(solution)/shard_map/pallas_call | solution.py:394
  207.8 1.9 slice_bitcast_fusion.4
  209.7 1.7 collective-permute-start.4
  211.5 2.0 collective-permute-start.6
  213.5 28.8 %shard_map.152.refs_3_ = f32[5,1024,256]{2,1,0:T(8,128)} custom-call(f32[8,5,128,256]{3,2,1,0:T(8,128)} %get-tuple-element.16.q.refs_2_, f32[1024,1024]{1,0:T(8,128)} %deriv.3, f32[1024,1024]{1,0:T(8,128)} %smooth.3), custom_call_target="tpu_custom_call" | custom-call | flops 16106127360 | bytes 52428800 | tf_op jit(solution)/shard_map/pallas_call | solution.py:367
  242.4 0.8 copy-done.9
  243.6 0.9 copy-done.12
  244.4 16.6 %shard_map.153 = f32[8,5,128,256]{3,2,1,0:T(8,128)} custom-call(f32[8,5,128,256]{3,2,1,0:T(8,128)} %all-to-all-done.q.refs_0_, f32[8,1,128,256]{3,2,1,0:T(8,128)} %copy-done.2, f32[8,5,128,256]{3,2,1,0:T(8,128)} %get-tuple-element.16.q.refs_2_, f32[5,1024,256]{2,1,0:T(8,128)} %shard_map.152.refs_3_, f32[5,256,128]{2,1,0:T(8,128)} %copy-done.9, ...), custom_call_target="tpu_custom_call" | custom-call | flops 10000000000 | bytes 52428800 | tf_op jit(solution)/shard_map/pallas_call | solution.py:405
  261.0 5.8 %all-to-all-start.2 = ((f32[8,5,128,256]{3,2,1,0:T(8,128)}), f32[8,5,128,256]{3,2,1,0:T(8,128)}, u32[]{:S(2)}, u32[]{:S(2)}) async-start(f32[8,5,128,256]{3,2,1,0:T(8,128)} %shard_map.153), calls=%async_computation.2 | async-start | bytes 10485760 | tf_op jit(solution)/shard_map/all_to_all | solution.py:360
  266.8 0.3 slice_reduce_fusion
  267.6 114.1 %all-to-all-done.2.refs_0_ = f32[8,5,128,256]{3,2,1,0:T(8,128)} async-done(((f32[8,5,128,256]{3,2,1,0:T(8,128)}), f32[8,5,128,256]{3,2,1,0:T(8,128)}, u32[]{:S(2)}, u32[]{:S(2)}) %all-to-all-start.2) | async-done | bytes 5242912 | tf_op jit(solution)/shard_map/all_to_all | solution.py:360
  381.8 1.1 slice.78
  383.4 1.9 fusion
  385.5 10.0 %all_to_all.25 = f32[8,8,128]{2,1,0:T(8,128)S(1)} all-to-all(f32[8,8,128]{2,1,0:T(8,128)S(1)} %convolution_bitcast_fusion), channel_id=1, replica_groups=mesh['gx'=8,'gz'=4] {'gx'}, dimensions={0} | all-to-all | bytes 65536 | tf_op jit(solution)/shard_map/all_to_all | solution.py:439
  395.5 0.6 broadcast_in_dim.18
  396.1 5.1 %all-to-all-start.4 = ((f32[4,8,128]{2,1,0:T(8,128)}), f32[4,8,128]{2,1,0:T(8,128)S(1)}, u32[]{:S(2)}, u32[]{:S(2)}) async-start(f32[4,8,128]{2,1,0:T(8,128)} %broadcast_in_dim.18), calls=%async_computation.4 | async-start | bytes 32768 | tf_op jit(solution)/shard_map/all_to_all | solution.py:444
  401.3 14.4 %shard_map.154 = (f32[2048,128]{1,0:T(8,128)}, f32[3,2048,128]{2,1,0:T(8,128)}, f32[2048,128]{1,0:T(8,128)}) custom-call(f32[8,5,128,256]{3,2,1,0:T(8,128)} %all-to-all-done.2.refs_0_), custom_call_target="tpu_custom_call" | custom-call | tf_op jit(solution)/shard_map/pallas_call | solution.py:416
  415.6 0.6 reduce_sum.19
  (50 shorter events, 2.1 us)
Async XLA Ops:
  0.6 384.7 %copy-start = (f32[256,128]{1,0:T(8,128)S(1)}, f32[256,128]{1,0:T(8,128)}, u32[]{:S(2)}) copy-start(f32[256,128]{1,0:T(8,128)} %param.20) | copy-start | bytes 393220
  13.6 12.4 %copy-start.8 = (s32[8]{0:T(128)S(1)}, s32[8]{0:T(128)}, u32[]{:S(2)}) copy-start(s32[8]{0:T(128)} %constant.39.clone) | copy-start | bytes 100
  13.6 121.4 %all-to-all-start = ((f32[8,5,128,256]{3,2,1,0:T(8,128)}), f32[8,5,128,256]{3,2,1,0:T(8,128)}, u32[]{:S(2)}, u32[]{:S(2)}) async-start(f32[8,5,128,256]{3,2,1,0:T(8,128)} %shard_map.148), calls=%async_computation | async-start | bytes 10485760 | tf_op jit(solution)/shard_map/all_to_all | solution.py:360
  135.0 49.9 %all-to-all-start.1 = ((f32[8,1,128,256]{3,2,1,0:T(8,128)}), f32[8,1,128,256]{3,2,1,0:T(8,128)S(1)}, u32[]{:S(2)}, u32[]{:S(2)}) async-start(f32[8,1,128,256]{3,2,1,0:T(8,128)} %shard_map.147), calls=%async_computation.1 | async-start | bytes 2097152 | tf_op jit(solution)/shard_map/all_to_all | solution.py:360
  152.0 32.9 %collective-permute-start = (f32[5,256,128]{2,1,0:T(8,128)S(1)}, f32[5,256,128]{2,1,0:T(8,128)S(1)}, u32[]{:S(2)}, u32[]{:S(2)}) collective-permute-start(f32[5,256,128]{2,1,0:T(8,128)S(1)} %get-tuple-element.29), channel_id=1, source_target_pairs={{0,8},{8,16},{16,24},{24,28},{28,20},{20,12},{12,4},{4,0},{1,9},{9... | collective-permute-start | bytes 1966088 | tf_op jit(solution)/shard_map/ppermute | solution.py:319
  153.5 31.4 %collective-permute-start.1 = (f32[5,256,128]{2,1,0:T(8,128)S(1)}, f32[5,256,128]{2,1,0:T(8,128)S(1)}, u32[]{:S(2)}, u32[]{:S(2)}) collective-permute-start(f32[5,256,128]{2,1,0:T(8,128)S(1)} %get-tuple-element.28), channel_id=1, source_target_pairs={{0,4},{8,0},{16,8},{24,16},{28,24},{20,28},{12,20},{4,12},{1,5},{9... | collective-permute-start | bytes 1966088 | tf_op jit(solution)/shard_map/ppermute | solution.py:320
  153.5 31.3 %collective-permute-start.2 = (f32[5,256,128]{2,1,0:T(8,128)S(1)}, f32[5,256,128]{2,1,0:T(8,128)S(1)}, u32[]{:S(2)}, u32[]{:S(2)}) collective-permute-start(f32[5,256,128]{2,1,0:T(8,128)S(1)} %get-tuple-element.27), channel_id=1, source_target_pairs={{0,1},{1,2},{2,3},{3,0},{4,5},{5,6},{6,7},{7,4},{8,9},{9,10},{10,1... | collective-permute-start | bytes 1966088 | tf_op jit(solution)/shard_map/ppermute | solution.py:321
  156.0 28.9 %collective-permute-start.3 = (f32[5,256,128]{2,1,0:T(8,128)S(1)}, f32[5,256,128]{2,1,0:T(8,128)}, u32[]{:S(2)}, u32[]{:S(2)}) collective-permute-start(f32[5,256,128]{2,1,0:T(8,128)S(1)} %get-tuple-element.26), channel_id=1, source_target_pairs={{0,3},{1,0},{2,1},{3,2},{4,7},{5,4},{6,5},{7,6},{8,11},{9,8},{10,9... | collective-permute-start | bytes 1966088 | tf_op jit(solution)/shard_map/ppermute | solution.py:322
  184.8 0.8 copy-start.3
  184.8 1.1 copy-start.4
  184.9 1.3 copy-start.5
  184.9 1.6 copy-start.2
  209.7 32.6 %collective-permute-start.4 = (f32[5,256,128]{2,1,0:T(8,128)S(1)}, f32[5,256,128]{2,1,0:T(8,128)S(1)}, u32[]{:S(2)}, u32[]{:S(2)}) collective-permute-start(f32[5,256,128]{2,1,0:T(8,128)S(1)} %get-tuple-element.25), channel_id=1, source_target_pairs={{0,8},{8,16},{16,24},{24,28},{28,20},{20,12},{12,4},{4,0},{1,9},{9... | collective-permute-start | bytes 1966088 | tf_op jit(solution)/shard_map/ppermute | solution.py:319
  211.4 30.9 %collective-permute-start.5 = (f32[5,256,128]{2,1,0:T(8,128)S(1)}, f32[5,256,128]{2,1,0:T(8,128)S(1)}, u32[]{:S(2)}, u32[]{:S(2)}) collective-permute-start(f32[5,256,128]{2,1,0:T(8,128)S(1)} %get-tuple-element.24), channel_id=1, source_target_pairs={{0,4},{8,0},{16,8},{24,16},{28,24},{20,28},{12,20},{4,12},{1,5},{9... | collective-permute-start | bytes 1966088 | tf_op jit(solution)/shard_map/ppermute | solution.py:320
  211.5 30.8 %collective-permute-start.6 = (f32[5,256,128]{2,1,0:T(8,128)S(1)}, f32[5,256,128]{2,1,0:T(8,128)S(1)}, u32[]{:S(2)}, u32[]{:S(2)}) collective-permute-start(f32[5,256,128]{2,1,0:T(8,128)S(1)} %get-tuple-element.23), channel_id=1, source_target_pairs={{0,1},{1,2},{2,3},{3,0},{4,5},{5,6},{6,7},{7,4},{8,9},{9,10},{10,1... | collective-permute-start | bytes 1966088 | tf_op jit(solution)/shard_map/ppermute | solution.py:321
  213.5 28.8 %collective-permute-start.7 = (f32[5,256,128]{2,1,0:T(8,128)S(1)}, f32[5,256,128]{2,1,0:T(8,128)S(1)}, u32[]{:S(2)}, u32[]{:S(2)}) collective-permute-start(f32[5,256,128]{2,1,0:T(8,128)S(1)} %get-tuple-element.22), channel_id=1, source_target_pairs={{0,3},{1,0},{2,1},{3,2},{4,7},{5,4},{6,5},{7,6},{8,11},{9,8},{10,9... | collective-permute-start | bytes 1966088 | tf_op jit(solution)/shard_map/ppermute | solution.py:322
  242.3 0.8 copy-start.9
  242.3 1.0 copy-start.10
  242.3 1.2 copy-start.11
  243.6 0.9 copy-start.12
  261.0 5.8 %copy-start.1 = (f32[128,16,128]{2,1,0:T(8,128)S(1)}, f32[128,16,128]{2,1,0:T(8,128)}, u32[]{:S(2)}) copy-start(f32[128,16,128]{2,1,0:T(8,128)} %param.15) | copy-start | bytes 3145732
  261.0 6.3 %copy-start.6 = (s32[128,16]{0,1:T(8,128)S(1)}, s32[128,16]{0,1:T(8,128)}, u32[]{:S(2)}) copy-start(s32[128,16]{0,1:T(8,128)} %param.18) | copy-start | bytes 24580
  261.0 6.4 %copy-start.7 = (s32[128,16]{0,1:T(8,128)S(1)}, s32[128,16]{0,1:T(8,128)}, u32[]{:S(2)}) copy-start(s32[128,16]{0,1:T(8,128)} %param.19) | copy-start | bytes 24580
  261.0 120.7 %all-to-all-start.2 = ((f32[8,5,128,256]{3,2,1,0:T(8,128)}), f32[8,5,128,256]{3,2,1,0:T(8,128)}, u32[]{:S(2)}, u32[]{:S(2)}) async-start(f32[8,5,128,256]{3,2,1,0:T(8,128)} %shard_map.153), calls=%async_computation.2 | async-start | bytes 10485760 | tf_op jit(solution)/shard_map/all_to_all | solution.py:360
  396.1 19.5 %all-to-all-start.4 = ((f32[4,8,128]{2,1,0:T(8,128)}), f32[4,8,128]{2,1,0:T(8,128)S(1)}, u32[]{:S(2)}, u32[]{:S(2)}) async-start(f32[4,8,128]{2,1,0:T(8,128)} %broadcast_in_dim.18), calls=%async_computation.4 | async-start | bytes 32768 | tf_op jit(solution)/shard_map/all_to_all | solution.py:444

commit v3 on v2

--- a/solution.py
+++ b/solution.py
@@ -138,20 +138,21 @@
                     target[pl.ds((first_row + row) * z_cells + half * count + k, 8, stride=z_cells), :] = planes[k]
 
 
-def matmul_kernel(half, parts, q, deriv, smooth, out, left_high, left_low, right_high, right_low):
+def matrices_kernel(deriv, smooth, left_high, left_low):
+    length = deriv.shape[0]
+
+    @pl.loop(0, length // 32)
+    def _(chunk):
+        row = pl.multiple_of(chunk * 32, 32)
+        for column, matrix, sign in ((0, smooth, 1.0), (1, deriv, -1.0)):
+            high, low = split2(sign * matrix[pl.ds(row, 32), :])
+            left_high[pl.ds(row, 32), column * length : (column + 1) * length] = high
+            left_low[pl.ds(row, 32), column * length : (column + 1) * length] = low
+
+
+def matmul_kernel(parts, q, left_high, left_low, out, right_high, right_low):
     blocks, _, x_cells, lanes = q.shape
     length = blocks * x_cells
-    span = x_cells // parts
-
-    @pl.loop(0, length // parts // 32)
-    def _(chunk):
-        row = pl.multiple_of(chunk * 32, 32)
-        source = pl.multiple_of(row // span * x_cells + half * span + row % span, 32)
-        for column, matrix, sign in ((0, smooth, 1.0), (1, deriv, -1.0)):
-            high, low = split2(sign * matrix[pl.ds(source, 32), :])
-            left_high[pl.ds(row, 32), column * length : (column + 1) * length] = high
-            left_low[pl.ds(row, 32), column * length : (column + 1) * length] = low
-
     step = 16
     for block in range(blocks):
 
@@ -360,20 +361,28 @@
         return lax.all_to_all(array, "gx", split_axis=0, concat_axis=0, tiled=True)
 
     start = swap(pack(FIELDS, density.reshape(flat), momentum.reshape((3,) + flat), energy.reshape(flat)))
-    packed_metric, start = lax.optimization_barrier((pack(1, metric.reshape(flat)), start))
+    left_high, left_low = pl.pallas_call(
+        matrices_kernel,
+        out_shape=(jax.ShapeDtypeStruct((length, 2 * length), BF16),) * 2,
+        in_specs=whole(2),
+        out_specs=tuple(whole(2)),
+        compiler_params=params(),
+    )(deriv_matrix, smooth_matrix)
+    packed_metric, left_high, left_low, start = lax.optimization_barrier(
+        (pack(1, metric.reshape(flat)), left_high, left_low, start)
+    )
     tile_metric = swap(packed_metric)
 
     def x_terms(state, half, parts):
         return pl.pallas_call(
-            functools.partial(matmul_kernel, half, parts),
+            functools.partial(matmul_kernel, parts),
             out_shape=jax.ShapeDtypeStruct((FIELDS, length // parts, lanes), F32),
             in_specs=whole(3),
             out_specs=whole(1)[0],
-            scratch_shapes=[pltpu.VMEM((length // parts, 2 * length), BF16)] * 2
-            + [pltpu.VMEM((FIELDS, 2 * length, lanes), BF16)] * 2,
+            scratch_shapes=[pltpu.VMEM((FIELDS, 2 * length, lanes), BF16)] * 2,
             compiler_params=params(),
             cost_estimate=cost(12 * FIELDS * length * length * lanes // parts, 40 * FIELDS * length * lanes),
-        )(state, deriv_matrix, smooth_matrix)
+        )(state, left_high, left_low)
 
     edge_shape = jax.ShapeDtypeStruct((4, FIELDS, length // 4, LANES), F32)
     place = jnp.asarray(order, jnp.int32)

time: 417 us -> 413 us (level)
  waiting for transfers between devices: 221 us -> 213 us
  Pallas kernels: 139 us -> 144 us
    all_to_all x3, waiting for transfers between devices: 221 us -> 213 us  [swap(): return lax.all_to_all(array, 'gx', split_axis=0, concat_axis=0, tiled=True)]
    pallas_call x2 -> x3, Pallas kernels: 57.6 us -> 62.5 us  [the longest x2 54.4 us: x_terms(): pl.pallas_call(functools.partial(matmul_kernel, parts), out_shape=jax.Sha...]
  transfers between devices with their start and end apart: 12 -> 12, of which waited for: 2 -> 2; matrix products, arithmetic and copies ran while one was open for 1% -> 1% of each run, Pallas kernels for 21% -> 23%
where the time goes in v3:
time: 413 us
  waiting for transfers between devices  213 us (52%)
  Pallas kernels  144 us (35%)
  starting transfers between devices  30 us (7%)
  local copies, waits for them, and re-layouts  10.5 us (3%)
  blocking collectives  9.98 us (2%)
    all_to_all x3, waiting for transfers between devices, swap(): return lax.all_to_all(array, 'gx', split_axis=0, concat_axis=0, tiled=True)  213 us
    pallas_call x2, Pallas kernels, x_terms(): pl.pallas_call(functools.partial(matmul_kernel, parts), out_shape=jax.Sha...  54.4 us
    pallas_call x1, Pallas kernels, body(): pl.pallas_call(functools.partial(finish_kernel, False, 0, 1), out_shape=(...  21.3 us
    pallas_call x2, Pallas kernels, pack(): pl.pallas_call(functools.partial(pack_kernel, count, z_cells, order), out...  18.8 us
    all_to_all x3, starting transfers between devices, swap(): return lax.all_to_all(array, 'gx', split_axis=0, concat_axis=0, tiled=True)  17 us
    pallas_call x1, Pallas kernels, body(): pl.pallas_call(functools.partial(finish_kernel, True, half, parts), out_s...  16.2 us
    pallas_call x1, Pallas kernels, body(): pl.pallas_call(functools.partial(unpack_kernel, count, z_cells, order), o...  14.4 us
    pallas_call x1, Pallas kernels, body(): pl.pallas_call(edge_kernel, out_shape=edge_shape, in_specs=whole(2), out_...  10.3 us
  transfers between devices with their start and end apart: 12, of which 2 were waited for; matrix products, arithmetic and copies ran while one was open for 1% of the time, Pallas kernels for 23%

profile of v3, /device:TPU:1, one launch (start us, length us, event | category | flops | bytes accessed | tf_op | source)
XLA Modules:
  0.0 412.6 jit_solution(9406064946889625815)
XLA Ops:
  0.6 12.9 %shard_map.149 = f32[8,5,128,256]{3,2,1,0:T(8,128)} custom-call(f32[2048,128]{1,0:T(8,128)} %bitcast.39, f32[3,2048,128]{2,1,0:T(8,128)} %bitcast.38, f32[2048,128]{1,0:T(8,128)} %bitcast.40), custom_call_target="tpu_custom_call" | custom-call | tf_op jit(solution)/shard_map/pallas_call | solution.py:352
  13.6 6.5 %all-to-all-start = ((f32[8,5,128,256]{3,2,1,0:T(8,128)}), f32[8,5,128,256]{3,2,1,0:T(8,128)}, u32[]{:S(2)}, u32[]{:S(2)}) async-start(f32[8,5,128,256]{3,2,1,0:T(8,128)} %shard_map.149), calls=%async_computation | async-start | bytes 10485760 | tf_op jit(solution)/shard_map/all_to_all | solution.py:361
  20.1 5.9 %shard_map.147 = f32[8,1,128,256]{3,2,1,0:T(8,128)} custom-call(f32[2048,128]{1,0:T(8,128)} %bitcast.37), custom_call_target="tpu_custom_call" | custom-call | tf_op jit(solution)/shard_map/pallas_call | solution.py:352
  26.0 0.7 compare_reduce_fusion
  27.9 8.1 %shard_map.148 = (bf16[1024,2048]{1,0:T(8,128)(2,1)}, bf16[1024,2048]{1,0:T(8,128)(2,1)}) custom-call(f32[1024,1024]{1,0:T(8,128)} %deriv.1, f32[1024,1024]{1,0:T(8,128)} %smooth.1), custom_call_target="tpu_custom_call" | custom-call | tf_op jit(solution)/shard_map/pallas_call | solution.py:364
  36.1 98.9 %all-to-all-done.q.refs_0_ = f32[8,5,128,256]{3,2,1,0:T(8,128)} async-done(((f32[8,5,128,256]{3,2,1,0:T(8,128)}), f32[8,5,128,256]{3,2,1,0:T(8,128)}, u32[]{:S(2)}, u32[]{:S(2)}) %all-to-all-start) | async-done | bytes 5242912 | tf_op jit(solution)/shard_map/all_to_all | solution.py:361
  135.0 4.7 %all-to-all-start.1 = ((f32[8,1,128,256]{3,2,1,0:T(8,128)}), f32[8,1,128,256]{3,2,1,0:T(8,128)S(1)}, u32[]{:S(2)}, u32[]{:S(2)}) async-start(f32[8,1,128,256]{3,2,1,0:T(8,128)} %shard_map.147), calls=%async_computation.1 | async-start | bytes 2097152 | tf_op jit(solution)/shard_map/all_to_all | solution.py:361
  139.7 10.3 %shard_map.151 = f32[4,5,256,128]{3,2,1,0:T(8,128)} custom-call(f32[8,5,128,256]{3,2,1,0:T(8,128)} %all-to-all-done.q.refs_0_, bf16[256,128]{1,0:T(8,128)(2,1)} %constant.37.clone.select.refs_9_), custom_call_target="tpu_custom_call" | custom-call | tf_op jit(solution)/shard_map/pallas_call | solution.py:394
  150.0 1.9 slice_bitcast_fusion
  151.9 1.5 collective-permute-start
  153.5 2.4 collective-permute-start.2
  156.0 27.2 %shard_map.150.refs_2_ = f32[5,1024,256]{2,1,0:T(8,128)} custom-call(f32[8,5,128,256]{3,2,1,0:T(8,128)} %all-to-all-done.q.refs_0_, bf16[1024,2048]{1,0:T(8,128)(2,1)} %get-tuple-element.21.left_high, bf16[1024,2048]{1,0:T(8,128)(2,1)} %get-tuple-element.22.left_low), custom_call_target="tpu_custom_call" | custom-call | flops 16106127360 | bytes 52428800 | tf_op jit(solution)/shard_map/pallas_call | solution.py:377
  183.2 0.7 iota.26.refs_7_.refs_8_
  184.5 0.3 copy-done.2
  184.8 21.3 %shard_map.152 = (f32[8,5,128,256]{3,2,1,0:T(8,128)}, f32[4,5,256,128]{3,2,1,0:T(8,128)}) custom-call(f32[8,5,128,256]{3,2,1,0:T(8,128)} %all-to-all-done.q.refs_0_, f32[8,1,128,256]{3,2,1,0:T(8,128)} %copy-done.2, f32[5,1024,256]{2,1,0:T(8,128)} %shard_map.150.refs_2_, f32[5,256,128]{2,1,0:T(8,128)} %copy-done.3, f32[5,256,128]{2,1,0:T(8,128)} %copy-done.4, ...), custom_call_target="tpu_custom_call" | custom-call | tf_op jit(solution)/shard_map/pallas_call | solution.py:403
  206.1 1.9 slice_bitcast_fusion.4
  208.0 1.7 collective-permute-start.4
  209.8 2.0 collective-permute-start.6
  211.9 27.2 %shard_map.153.refs_3_ = f32[5,1024,256]{2,1,0:T(8,128)} custom-call(f32[8,5,128,256]{3,2,1,0:T(8,128)} %get-tuple-element.24.q.refs_2_, bf16[1024,2048]{1,0:T(8,128)(2,1)} %get-tuple-element.21.left_high, bf16[1024,2048]{1,0:T(8,128)(2,1)} %get-tuple-element.22.left_low), custom_call_target="tpu_custom_call" | custom-call | flops 16106127360 | bytes 52428800 | tf_op jit(solution)/shard_map/pallas_call | solution.py:377
  239.1 0.8 copy-done.9
  240.3 0.9 copy-done.12
  241.2 16.2 %shard_map.154 = f32[8,5,128,256]{3,2,1,0:T(8,128)} custom-call(f32[8,5,128,256]{3,2,1,0:T(8,128)} %all-to-all-done.q.refs_0_, f32[8,1,128,256]{3,2,1,0:T(8,128)} %copy-done.2, f32[8,5,128,256]{3,2,1,0:T(8,128)} %get-tuple-element.24.q.refs_2_, f32[5,1024,256]{2,1,0:T(8,128)} %shard_map.153.refs_3_, f32[5,256,128]{2,1,0:T(8,128)} %copy-done.9, ...), custom_call_target="tpu_custom_call" | custom-call | flops 10000000000 | bytes 52428800 | tf_op jit(solution)/shard_map/pallas_call | solution.py:414
  257.4 5.8 %all-to-all-start.2 = ((f32[8,5,128,256]{3,2,1,0:T(8,128)}), f32[8,5,128,256]{3,2,1,0:T(8,128)}, u32[]{:S(2)}, u32[]{:S(2)}) async-start(f32[8,5,128,256]{3,2,1,0:T(8,128)} %shard_map.154), calls=%async_computation.2 | async-start | bytes 10485760 | tf_op jit(solution)/shard_map/all_to_all | solution.py:361
  263.2 0.3 slice_reduce_fusion
  264.0 114.1 %all-to-all-done.2.refs_0_ = f32[8,5,128,256]{3,2,1,0:T(8,128)} async-done(((f32[8,5,128,256]{3,2,1,0:T(8,128)}), f32[8,5,128,256]{3,2,1,0:T(8,128)}, u32[]{:S(2)}, u32[]{:S(2)}) %all-to-all-start.2) | async-done | bytes 5242912 | tf_op jit(solution)/shard_map/all_to_all | solution.py:361
  378.1 1.1 slice.78
  379.8 1.9 fusion
  381.9 10.0 %all_to_all.25 = f32[8,8,128]{2,1,0:T(8,128)S(1)} all-to-all(f32[8,8,128]{2,1,0:T(8,128)S(1)} %convolution_bitcast_fusion), channel_id=1, replica_groups=mesh['gx'=8,'gz'=4] {'gx'}, dimensions={0} | all-to-all | bytes 65536 | tf_op jit(solution)/shard_map/all_to_all | solution.py:448
  391.9 0.6 broadcast_in_dim.18
  392.5 5.1 %all-to-all-start.4 = ((f32[4,8,128]{2,1,0:T(8,128)}), f32[4,8,128]{2,1,0:T(8,128)S(1)}, u32[]{:S(2)}, u32[]{:S(2)}) async-start(f32[4,8,128]{2,1,0:T(8,128)} %broadcast_in_dim.18), calls=%async_computation.4 | async-start | bytes 32768 | tf_op jit(solution)/shard_map/all_to_all | solution.py:453
  397.7 14.4 %shard_map.155 = (f32[2048,128]{1,0:T(8,128)}, f32[3,2048,128]{2,1,0:T(8,128)}, f32[2048,128]{1,0:T(8,128)}) custom-call(f32[8,5,128,256]{3,2,1,0:T(8,128)} %all-to-all-done.2.refs_0_), custom_call_target="tpu_custom_call" | custom-call | tf_op jit(solution)/shard_map/pallas_call | solution.py:425
  412.0 0.6 reduce_sum.19
  (51 shorter events, 2.3 us)
Async XLA Ops:
  0.6 381.1 %copy-start = (f32[256,128]{1,0:T(8,128)S(1)}, f32[256,128]{1,0:T(8,128)}, u32[]{:S(2)}) copy-start(f32[256,128]{1,0:T(8,128)} %param.20) | copy-start | bytes 393220
  13.6 12.4 %copy-start.8 = (s32[8]{0:T(128)S(1)}, s32[8]{0:T(128)}, u32[]{:S(2)}) copy-start(s32[8]{0:T(128)} %constant.39.clone) | copy-start | bytes 100
  13.6 121.4 %all-to-all-start = ((f32[8,5,128,256]{3,2,1,0:T(8,128)}), f32[8,5,128,256]{3,2,1,0:T(8,128)}, u32[]{:S(2)}, u32[]{:S(2)}) async-start(f32[8,5,128,256]{3,2,1,0:T(8,128)} %shard_map.149), calls=%async_computation | async-start | bytes 10485760 | tf_op jit(solution)/shard_map/all_to_all | solution.py:361
  135.0 48.2 %all-to-all-start.1 = ((f32[8,1,128,256]{3,2,1,0:T(8,128)}), f32[8,1,128,256]{3,2,1,0:T(8,128)S(1)}, u32[]{:S(2)}, u32[]{:S(2)}) async-start(f32[8,1,128,256]{3,2,1,0:T(8,128)} %shard_map.147), calls=%async_computation.1 | async-start | bytes 2097152 | tf_op jit(solution)/shard_map/all_to_all | solution.py:361
  151.9 31.2 %collective-permute-start = (f32[5,256,128]{2,1,0:T(8,128)S(1)}, f32[5,256,128]{2,1,0:T(8,128)S(1)}, u32[]{:S(2)}, u32[]{:S(2)}) collective-permute-start(f32[5,256,128]{2,1,0:T(8,128)S(1)} %get-tuple-element.37), channel_id=1, source_target_pairs={{0,8},{8,16},{16,24},{24,28},{28,20},{20,12},{12,4},{4,0},{1,9},{9... | collective-permute-start | bytes 1966088 | tf_op jit(solution)/shard_map/ppermute | solution.py:320
  153.5 29.7 %collective-permute-start.1 = (f32[5,256,128]{2,1,0:T(8,128)S(1)}, f32[5,256,128]{2,1,0:T(8,128)S(1)}, u32[]{:S(2)}, u32[]{:S(2)}) collective-permute-start(f32[5,256,128]{2,1,0:T(8,128)S(1)} %get-tuple-element.36), channel_id=1, source_target_pairs={{0,4},{8,0},{16,8},{24,16},{28,24},{20,28},{12,20},{4,12},{1,5},{9... | collective-permute-start | bytes 1966088 | tf_op jit(solution)/shard_map/ppermute | solution.py:321
  153.5 29.7 %collective-permute-start.2 = (f32[5,256,128]{2,1,0:T(8,128)S(1)}, f32[5,256,128]{2,1,0:T(8,128)S(1)}, u32[]{:S(2)}, u32[]{:S(2)}) collective-permute-start(f32[5,256,128]{2,1,0:T(8,128)S(1)} %get-tuple-element.35), channel_id=1, source_target_pairs={{0,1},{1,2},{2,3},{3,0},{4,5},{5,6},{6,7},{7,4},{8,9},{9,10},{10,1... | collective-permute-start | bytes 1966088 | tf_op jit(solution)/shard_map/ppermute | solution.py:322
  156.0 27.2 %collective-permute-start.3 = (f32[5,256,128]{2,1,0:T(8,128)S(1)}, f32[5,256,128]{2,1,0:T(8,128)}, u32[]{:S(2)}, u32[]{:S(2)}) collective-permute-start(f32[5,256,128]{2,1,0:T(8,128)S(1)} %get-tuple-element.34), channel_id=1, source_target_pairs={{0,3},{1,0},{2,1},{3,2},{4,7},{5,4},{6,5},{7,6},{8,11},{9,8},{10,9... | collective-permute-start | bytes 1966088 | tf_op jit(solution)/shard_map/ppermute | solution.py:323
  183.2 0.8 copy-start.3
  183.2 1.1 copy-start.4
  183.2 1.3 copy-start.5
  183.2 1.6 copy-start.2
  208.0 31.0 %collective-permute-start.4 = (f32[5,256,128]{2,1,0:T(8,128)S(1)}, f32[5,256,128]{2,1,0:T(8,128)S(1)}, u32[]{:S(2)}, u32[]{:S(2)}) collective-permute-start(f32[5,256,128]{2,1,0:T(8,128)S(1)} %get-tuple-element.33), channel_id=1, source_target_pairs={{0,8},{8,16},{16,24},{24,28},{28,20},{20,12},{12,4},{4,0},{1,9},{9... | collective-permute-start | bytes 1966088 | tf_op jit(solution)/shard_map/ppermute | solution.py:320
  209.8 29.3 %collective-permute-start.5 = (f32[5,256,128]{2,1,0:T(8,128)S(1)}, f32[5,256,128]{2,1,0:T(8,128)S(1)}, u32[]{:S(2)}, u32[]{:S(2)}) collective-permute-start(f32[5,256,128]{2,1,0:T(8,128)S(1)} %get-tuple-element.32), channel_id=1, source_target_pairs={{0,4},{8,0},{16,8},{24,16},{28,24},{20,28},{12,20},{4,12},{1,5},{9... | collective-permute-start | bytes 1966088 | tf_op jit(solution)/shard_map/ppermute | solution.py:321
  209.8 29.2 %collective-permute-start.6 = (f32[5,256,128]{2,1,0:T(8,128)S(1)}, f32[5,256,128]{2,1,0:T(8,128)S(1)}, u32[]{:S(2)}, u32[]{:S(2)}) collective-permute-start(f32[5,256,128]{2,1,0:T(8,128)S(1)} %get-tuple-element.31), channel_id=1, source_target_pairs={{0,1},{1,2},{2,3},{3,0},{4,5},{5,6},{6,7},{7,4},{8,9},{9,10},{10,1... | collective-permute-start | bytes 1966088 | tf_op jit(solution)/shard_map/ppermute | solution.py:322
  211.8 27.2 %collective-permute-start.7 = (f32[5,256,128]{2,1,0:T(8,128)S(1)}, f32[5,256,128]{2,1,0:T(8,128)S(1)}, u32[]{:S(2)}, u32[]{:S(2)}) collective-permute-start(f32[5,256,128]{2,1,0:T(8,128)S(1)} %get-tuple-element.30), channel_id=1, source_target_pairs={{0,3},{1,0},{2,1},{3,2},{4,7},{5,4},{6,5},{7,6},{8,11},{9,8},{10,9... | collective-permute-start | bytes 1966088 | tf_op jit(solution)/shard_map/ppermute | solution.py:323
  239.0 0.8 copy-start.9
  239.1 1.0 copy-start.10
  239.1 1.2 copy-start.11
  240.3 0.9 copy-start.12
  257.4 5.8 %copy-start.1 = (f32[128,16,128]{2,1,0:T(8,128)S(1)}, f32[128,16,128]{2,1,0:T(8,128)}, u32[]{:S(2)}) copy-start(f32[128,16,128]{2,1,0:T(8,128)} %param.15) | copy-start | bytes 3145732
  257.4 6.2 %copy-start.6 = (s32[128,16]{0,1:T(8,128)S(1)}, s32[128,16]{0,1:T(8,128)}, u32[]{:S(2)}) copy-start(s32[128,16]{0,1:T(8,128)} %param.18) | copy-start | bytes 24580
  257.4 6.4 %copy-start.7 = (s32[128,16]{0,1:T(8,128)S(1)}, s32[128,16]{0,1:T(8,128)}, u32[]{:S(2)}) copy-start(s32[128,16]{0,1:T(8,128)} %param.19) | copy-start | bytes 24580
  257.4 120.7 %all-to-all-start.2 = ((f32[8,5,128,256]{3,2,1,0:T(8,128)}), f32[8,5,128,256]{3,2,1,0:T(8,128)}, u32[]{:S(2)}, u32[]{:S(2)}) async-start(f32[8,5,128,256]{3,2,1,0:T(8,128)} %shard_map.154), calls=%async_computation.2 | async-start | bytes 10485760 | tf_op jit(solution)/shard_map/all_to_all | solution.py:361
  392.5 19.5 %all-to-all-start.4 = ((f32[4,8,128]{2,1,0:T(8,128)}), f32[4,8,128]{2,1,0:T(8,128)S(1)}, u32[]{:S(2)}, u32[]{:S(2)}) async-start(f32[4,8,128]{2,1,0:T(8,128)} %broadcast_in_dim.18), calls=%async_computation.4 | async-start | bytes 32768 | tf_op jit(solution)/shard_map/all_to_all | solution.py:453
